TPU v7x, 256 devices: a whole 4x4x8 slice. The times are simulated.
256 devices in a mesh: batch: 64 (over x, z, core), proto: 4 (over y).
Axes of the slice: x: 4, y: 4, z: 8, core: 2. Of those that a mesh axis runs over, the one named last changes fastest.
Arguments:
- teacher_tokens: bfloat16 [512, 256, 256], P('batch'), may hold values from -36 to 36
- student_tokens: bfloat16 [512, 256, 256], P('batch'), may hold values from -36 to 36
- masked_index: int32 [512, 64], P('batch'), may hold values from 0 to 255, as said below
- prototypes: bfloat16 [32768, 256], P(('batch', 'proto')), may hold values from -0.375 to 0.375
Outputs:
- loss: float32 [], replicated
- grad_student: bfloat16 [32768, 256], P('batch')
- grad_weight: float32 [32768, 256], P(('batch', 'proto'))
Inputs may be any that keep to these rules, and one draw needn't show every extreme that they name: `masked_index`: each row holds 64 distinct patch positions of its image.
All inputs are finite; a program needn't handle non-finite values.
Results may differ from a plain program's by a relative error of at most 0.0049.
Values may be sent and summed in bfloat16 or wider, within the bound.
No kernel may reach another device: no remote copies, remote signals or barrier semaphores. Data moves between devices by JAX's collectives and lax.ppermute only.
A program may use at most 128 MiB of HBM per device.

v0:
```python
import jax
import jax.numpy as jnp
from jax import lax
from jax.sharding import PartitionSpec as P

ITERS = 3


def column_scale(partial_value):
    return 1.0 / lax.psum(partial_value, "batch")


def row_scale(kern, col_scale):
    return 1.0 / lax.psum(jnp.sum(kern * col_scale[None, :], axis=1), "proto")


def body(teacher_tokens, student_tokens, masked_index, prototypes):
    index = masked_index[:, :, None]
    width = teacher_tokens.shape[2]
    teacher_rows = jnp.take_along_axis(teacher_tokens, index, axis=1).reshape(-1, width)
    student_rows = jnp.take_along_axis(student_tokens, index, axis=1).reshape(-1, width)
    local_rows = teacher_rows.shape[0]
    total_rows = local_rows * lax.axis_size("batch")
    stacked = jnp.concatenate([teacher_rows, student_rows], axis=0)
    contract = (((1,), (1,)), ((), ()))
    gathered = lax.all_gather(prototypes, "batch", axis=0, tiled=True)
    scores = lax.dot_general(stacked, gathered, contract, preferred_element_type=jnp.float32)
    teacher_scores = scores[:local_rows] * (1.0 / 0.07)
    student_scores = scores[local_rows:] * (1.0 / 0.1)
    teacher_top, student_top = lax.pmax(
        (jnp.max(teacher_scores, axis=1), jnp.max(student_scores, axis=1)), "proto"
    )
    kern = jnp.exp(teacher_scores - teacher_top[:, None])
    col_scale = column_scale(jnp.sum(kern, axis=0))
    for step in range(ITERS - 1):
        rows_now = row_scale(kern, col_scale)
        col_scale = column_scale(jnp.sum(kern * rows_now[:, None], axis=0))
    shifted = student_scores - student_top[:, None]
    target_sums, totals = lax.psum(
        (jnp.sum(kern * col_scale[None, :], axis=1), jnp.sum(jnp.exp(shifted), axis=1)), "proto"
    )
    targets = (1.0 / target_sums)[:, None] * kern * col_scale[None, :]
    log_probs = shifted - jnp.log(totals)[:, None]
    loss = lax.psum(-jnp.sum(targets * log_probs), ("batch", "proto")) / total_rows
    grad_logits = ((jnp.exp(log_probs) - targets) / (0.1 * total_rows)).astype(jnp.bfloat16)
    partial_grad = jnp.dot(grad_logits, gathered, preferred_element_type=jnp.float32)
    grad_student = lax.psum(partial_grad, "proto").astype(jnp.bfloat16)
    grad_weight = lax.psum_scatter(
        lax.dot_general(
            grad_logits, student_rows, (((0,), (0,)), ((), ())), preferred_element_type=jnp.float32
        ),
        "batch",
        scatter_dimension=0,
        tiled=True,
    )
    return (loss, grad_student, grad_weight)


def solution(mesh):
    placed = (
        P("batch", None, None),
        P("batch", None, None),
        P("batch", None),
        P(("batch", "proto"), None),
    )
    return jax.shard_map(
        body,
        mesh=mesh,
        in_specs=placed,
        out_specs=(P(), P("batch", None), P(("batch", "proto"), None)),
        check_vma=False,
    )
```

profile of v0, /device:TPU:8, one launch (start us, length us, event | category | flops | bytes accessed | tf_op | source)
XLA Modules:
  0.0 1131.0 jit_solution(9820427183723715192)
XLA Ops:
  7.2 0.7 all-gather.2.cloned.1.call-update
  7.9 0.0 reduce-scatter.2.cloned.1.call-start
  8.0 0.7 shift-left_or_fusion
  8.7 0.1 reshape.36
  8.7 3.2 gather_fusion.1
  11.9 7.0 gather_fusion
  18.9 0.7 and_bitcast_fusion
  19.6 0.1 broadcast_select_fusion.1
  19.8 72.9 %all-gather.2.cloned.1.call-done = bf16[8192,256]{1,0:T(8,128)(2,1)} async-done(((bf16[128,256]{1,0:T(8,128)(2,1)}), bf16[8192,256]{1,0:T(8,128)(2,1)}) %all-gather.2.cloned.1.call-update) | async-done | bytes 4194320 | tf_op jit(solution)/shard_map/all_gather | solution.py:26
  92.7 15.6 %fusion.3 = f32[1024,8192]{1,0:T(8,128)} fusion(bf16[8192,256]{1,0:T(8,128)(2,1)} %all-gather.2.cloned.1.call-done, bf16[512,256]{1,0:T(8,128)(2,1)S(1)} %bitcast.20, bf16[512,256]{1,0:T(8,128)(2,1)S(1)} %bitcast.24), kind=kOutput, calls=%fused_computation.17 | convolution fusion | flops 4296015872 | bytes 38273024 | tf_op jit(solution)/shard_map/dot_general | solution.py:27
  108.3 7.2 fusion
  115.5 8.6 pmax.14
  124.1 7.5 fusion.8
  131.6 246.4 %psum.63 = f32[8192]{0:T(1024)S(1)} all-reduce(f32[8192]{0:T(1024)S(1)} %fusion.8), channel_id=1, replica_groups=mesh['batch'=64,'proto'=4] {'batch'}, use_global_device_ids=true, to_apply=%region_3.0 | all-reduce | flops 8192 | bytes 65536 | tf_op jit(solution)/shard_map/psum | solution.py:10
  378.1 7.9 multiply_reduce_fusion.5
  386.0 10.1 psum.64
  396.1 7.8 multiply_reduce_fusion.4
  404.0 246.1 %psum.65 = f32[8192]{0:T(1024)S(1)} all-reduce(f32[8192]{0:T(1024)S(1)} %multiply_reduce_fusion.4), channel_id=1, replica_groups=mesh['batch'=64,'proto'=4] {'batch'}, use_global_device_ids=true, to_apply=%region_7.0 | all-reduce | flops 8192 | bytes 65536 | tf_op jit(solution)/shard_map/psum | solution.py:10
  650.1 7.9 multiply_reduce_fusion.3
  658.1 8.0 psum.66
  666.0 12.1 %multiply_reduce_fusion.2 = (f32[8192]{0:T(1024)S(1)}, f32[512]{0:T(512)S(1)}) fusion(f32[512]{0:T(512)S(1)} %broadcast_divide_fusion.4, f32[512]{0:T(512)S(1)} %pmax.14, f32[1024,8192]{1,0:T(8,128)} %fusion.3), kind=kLoop, calls=%fused_computation.9 | loop fusion | flops 25157120 | bytes 33593344 | tf_op jit(solution)/shard_map/reduce_sum | solution.py:37
  678.1 246.1 %psum.67 = f32[8192]{0:T(1024)S(1)} all-reduce(f32[8192]{0:T(1024)S(1)} %get-tuple-element.6), channel_id=1, replica_groups=mesh['batch'=64,'proto'=4] {'batch'}, use_global_device_ids=true, to_apply=%region_11.0 | all-reduce | flops 8192 | bytes 65536 | tf_op jit(solution)/shard_map/psum | solution.py:10
  924.3 9.7 pmax.15
  934.0 12.8 %multiply_reduce_fusion.1 = (f32[512]{0:T(512)S(1)}, f32[512]{0:T(512)S(1)}) fusion(f32[8192]{0:T(1024)S(1)} %broadcast_divide_fusion, f32[512]{0:T(512)S(1)} %pmax.14, f32[1024,8192]{1,0:T(8,128)} %fusion.3, f32[512]{0:T(512)S(1)} %pmax.15), kind=kLoop, calls=%fused_computation.8 | loop fusion | flops 29359104 | bytes 33595392 | tf_op jit(solution)/shard_map/reduce_sum | solution.py:40
  946.8 7.8 all-reduce
  954.6 15.1 %multiply_convert_fusion = (bf16[512,8192]{1,0:T(8,128)(2,1)S(1)}, f32[]{:T(128)}) fusion(f32[1024,8192]{1,0:T(8,128)} %fusion.3, f32[512]{0:T(512)S(1)} %log.3, f32[512]{0:T(512)S(1)} %pmax.15, f32[512]{0:T(512)S(1)} %broadcast_divide_fusion.3, f32[8192]{0:T(1024)S(1)} %broadcast_divide_fusion, f32[512]{0:T(512)S(1)} %pmax.14), kind=kLoop, calls=%fused_computation.4 | loop fusion | flops 50331648 | bytes 41984004 | tf_op jit(solution)/shard_map/convert_element_type | solution.py:45
  969.7 3.2 copy-done.1
  972.9 5.6 fusion.10
  979.1 72.6 %psum.70 = f32[]{:T(128)} all-reduce(f32[]{:T(128)S(6)} %neg.3), channel_id=1, replica_groups=mesh['batch'=64,'proto'=4] {'batch','proto'}, use_global_device_ids=true, to_apply=%region_19.0 | all-reduce | flops 1 | bytes 8 | tf_op jit(solution)/shard_map/psum | solution.py:44
  1051.8 6.9 fusion.9
  1059.3 20.4 %all-reduce.2 = bf16[512,256]{1,0:T(8,128)(2,1)} all-reduce(f32[512,256]{1,0:T(8,128)S(1)} %fusion.9), channel_id=1, replica_groups=mesh['batch'=64,'proto'=4] {'proto'}, use_global_device_ids=true, to_apply=%region_20.0 | all-reduce | flops 131072 | bytes 786432 | tf_op jit(solution)/shard_map/psum | solution.py:47
  1079.7 43.3 %reduce-scatter.2.cloned.1.call-done = f32[128,256]{1,0:T(8,128)} async-done(((f32[8192,256]{1,0:T(8,128)}), f32[128,256]{1,0:T(8,128)}) %reduce-scatter.2.cloned.1.call-update) | async-done | bytes 131088 | tf_op jit(solution)/shard_map/reduce_scatter | solution.py:48
  (12 shorter events, 0.1 us)
Async XLA Ops:
  7.2 1.6 copy-start
  7.2 85.5 %all-gather.2.cloned.1.call-start = ((), (), s32[]{:S(2)}) async-start(), calls=%async_computation.1 | async-start | bytes 4259840 | tf_op jit(solution)/shard_map/all_gather | solution.py:26
  7.9 1115.1 %reduce-scatter.2.cloned.1.call-start = ((), (), s32[]{:S(2)}) async-start(), calls=%async_computation.2 | async-start | bytes 8519680 | tf_op jit(solution)/shard_map/reduce_scatter | solution.py:48
  969.7 3.2 copy-start.1
Sparse Core Ops, SparseCore 0:
  10.8 81.8 all-gather.1
  978.6 144.3 reduce-scatter.1
where the time goes:
time: 1130 us
  blocking collectives  876 us (78%)
  waiting for transfers between devices  117 us (10%)
  other arithmetic  80 us (7%)
  matrix products  28.1 us (2%)
  between operations  16.5 us (1%)
  local copies, waits for them, and re-layouts  13.5 us (1%)
    psum x3, blocking collectives, column_scale(): return 1.0 / lax.psum(partial_value, 'batch')  739 us
    all_gather x1, waiting for transfers between devices, body(): gathered = lax.all_gather(prototypes, 'batch', axis=0, tiled=True)  72.9 us
    psum x1, blocking collectives, body(): lax.psum(-jnp.sum(targets * log_probs), ('batch', 'proto')) / total_rows  72.6 us
    reduce_scatter x1, waiting for transfers between devices, body(): lax.psum_scatter(lax.dot_general(grad_logits, student_rows, (((0,), (0,))...  43.3 us
  transfers between devices with their start and end apart: 2, of which 2 were waited for; matrix products, arithmetic and copies ran while one was open for 2% of the time, Pallas kernels for 0%

commit v1 on v0

v1 whole, which is shorter than its diff:
```python
import functools

import jax
import jax.numpy as jnp
from jax import lax
from jax.experimental import pallas as pl
from jax.experimental.pallas import tpu as pltpu
from jax.sharding import Mesh, PartitionSpec as P

X, Z, C, Y = 4, 8, 2, 4
F32, BF16 = jnp.float32, jnp.bfloat16
D = 256
IMAGES = 8
MASKED = 64
OWN_ROWS = 512
OWN_PROTOS = 128
ROWS = X * OWN_ROWS
PROTOS = Z * C * OWN_PROTOS
TOTAL_ROWS = ROWS * Z * C
PEERS = X * Y
LANES = 128
GROUPS = 16
BLOCK = 256
HALVES = BLOCK // LANES
T_SCALE = 1.0 / 0.07
S_SCALE = 1.0 / 0.1
MIB = 1 << 20
TRANS_B = (((1,), (1,)), ((), ()))


def whole(shape):
    return pl.BlockSpec(shape, lambda *_: (0,) * len(shape))


def params(mib=32):
    return pltpu.CompilerParams(vmem_limit_bytes=mib * MIB, dimension_semantics=("arbitrary",))


def down(row):
    return jnp.transpose(jnp.broadcast_to(row, (LANES, LANES)))


def along(column_parts):
    return jnp.sum(jnp.transpose(column_parts), axis=0, keepdims=True)


def spread(ref, first, at, row):
    ref[:, pl.ds(first + at, 1), :] = jnp.broadcast_to(row[None], (ref.shape[0], 1, LANES))


def pick_kernel(index_ref, tokens_ref, out_ref):
    for image in range(IMAGES):
        at = lax.broadcasted_iota(jnp.int32, (D, MASKED), 0)
        chosen = (at == index_ref[image : image + 1, :]).astype(BF16)
        rows = lax.dot_general(
            chosen, tokens_ref[image], (((0,), (0,)), ((), ())), preferred_element_type=F32
        )
        out_ref[image * MASKED : (image + 1) * MASKED, :] = rows.astype(BF16)


def pick_rows(index, tokens):
    return pl.pallas_call(
        pick_kernel,
        out_shape=jax.ShapeDtypeStruct((OWN_ROWS, D), BF16),
        in_specs=[whole(index.shape), whole(tokens.shape)],
        out_specs=whole((OWN_ROWS, D)),
        grid=(1,),
        compiler_params=params(),
        name="pick_rows",
    )(index, tokens)


def place(pos_ref, pieces, out_ref, first=0, valid_ref=None):
    for number, piece in enumerate(pieces):
        size = piece.shape[0]
        at = pl.multiple_of(pos_ref[first + number] * size, size)
        if valid_ref is None:
            out_ref[pl.ds(at, size), :] = piece[...]
        else:
            @pl.when(valid_ref[number] == 1)
            def _(piece=piece, at=at, size=size):
                out_ref[pl.ds(at, size), :] = piece[...]


def teacher_kernel(xpos, wpos, wvalid, *refs):
    rows_in, protos_in = refs[:X], refs[X : X + 9]
    kern_ref, top_ref, tops_ref, protos_ref, rows_ref = refs[X + 9 :]
    step = pl.program_id(0)

    @pl.when(step == 0)
    def _():
        place(xpos, rows_in, rows_ref)
        place(wpos, protos_in, protos_ref, valid_ref=wvalid)

    rows = rows_ref[pl.ds(pl.multiple_of(step * BLOCK, BLOCK), BLOCK), :]
    scores = lax.dot_general(rows, protos_ref[...], TRANS_B, preferred_element_type=F32) * T_SCALE
    top = jnp.max(scores, axis=1, keepdims=True)
    kern_ref[...] = jnp.exp(scores - top).astype(BF16)
    for half in range(HALVES):
        part = jnp.broadcast_to(top[half * LANES : (half + 1) * LANES], (LANES, LANES))
        row = jnp.transpose(part)[0:1, :]
        top_ref[pl.ds(step * HALVES + half, 1), :] = row
        spread(tops_ref, 0, step * HALVES + half, row)


def teacher_scores(xpos, wpos, wvalid, rows, protos):
    return pl.pallas_call(
        teacher_kernel,
        out_shape=(
            jax.ShapeDtypeStruct((ROWS, PROTOS), BF16),
            jax.ShapeDtypeStruct((GROUPS, LANES), F32),
            jax.ShapeDtypeStruct((PEERS, GROUPS, LANES), F32),
            jax.ShapeDtypeStruct((PROTOS, D), BF16),
        ),
        grid_spec=pltpu.PrefetchScalarGridSpec(
            num_scalar_prefetch=3,
            grid=(ROWS // BLOCK,),
            in_specs=[whole(a.shape) for a in rows + protos],
            out_specs=(
                pl.BlockSpec((BLOCK, PROTOS), lambda i, *_: (i, 0)),
                whole((GROUPS, LANES)),
                whole((PEERS, GROUPS, LANES)),
                whole((PROTOS, D)),
            ),
            scratch_shapes=[pltpu.VMEM((ROWS, D), BF16)],
        ),
        compiler_params=params(),
        name="teacher_scores",
    )(xpos, wpos, wvalid, *rows, *protos)


def student_kernel(xpos, *refs):
    rows_in, protos_ref = refs[:X], refs[X]
    rows_ref, lse_ref = refs[X + 1 :]
    step = pl.program_id(0)

    @pl.when(step == 0)
    def _():
        place(xpos, rows_in, rows_ref)

    rows = rows_ref[pl.ds(pl.multiple_of(step * BLOCK, BLOCK), BLOCK), :]
    scores = lax.dot_general(rows, protos_ref[...], TRANS_B, preferred_element_type=F32) * S_SCALE
    top = jnp.max(scores, axis=1, keepdims=True)
    lse = top + jnp.log(jnp.sum(jnp.exp(scores - top), axis=1, keepdims=True))
    for half in range(HALVES):
        part = jnp.broadcast_to(lse[half * LANES : (half + 1) * LANES], (LANES, LANES))
        lse_ref[pl.ds(step * HALVES + half, 1), :] = jnp.transpose(part)[0:1, :]


def student_totals(xpos, rows, protos):
    return pl.pallas_call(
        student_kernel,
        out_shape=(
            jax.ShapeDtypeStruct((ROWS, D), BF16),
            jax.ShapeDtypeStruct((GROUPS, LANES), F32),
        ),
        grid_spec=pltpu.PrefetchScalarGridSpec(
            num_scalar_prefetch=1,
            grid=(ROWS // BLOCK,),
            in_specs=[whole(a.shape) for a in rows] + [whole((PROTOS, D))],
            out_specs=(whole((ROWS, D)), whole((GROUPS, LANES))),
        ),
        compiler_params=params(),
        name="student_totals",
    )(xpos, *rows, protos)


def row_weight(first, weight_ref, got_ref, top_ref, out_ref):
    if first:
        got = got_ref[0]
        for peer in range(1, PEERS):
            got = jnp.maximum(got, got_ref[peer])
        out_ref[...] = jnp.exp(top_ref[...] - got)
    else:
        out_ref[...] = weight_ref[...] / jnp.sum(got_ref[:, :GROUPS, :], axis=0)


def column_kernel(first, own_ref, got_ref, kern_ref, sums_ref, weight_ref, acc_ref):
    step = pl.program_id(0)

    @pl.when(step == 0)
    def _():
        row_weight(first, own_ref, got_ref, own_ref, weight_ref)
        acc_ref[...] = jnp.zeros_like(acc_ref)

    for half in range(HALVES):
        weight = down(weight_ref[pl.ds(step * HALVES + half, 1), :])
        for group in range(GROUPS):
            part = kern_ref[half * LANES : (half + 1) * LANES, group * LANES : (group + 1) * LANES]
            part = (part.astype(F32) * weight).reshape(LANES // 8, 8, LANES)
            acc_ref[group] += jnp.sum(part, axis=0)

    @pl.when(step == pl.num_programs(0) - 1)
    def _():
        for group in range(GROUPS):
            sums_ref[group : group + 1, :] = jnp.sum(acc_ref[group], axis=0, keepdims=True)


def column_pass(first, own, got, kern):
    return pl.pallas_call(
        functools.partial(column_kernel, first),
        out_shape=(
            jax.ShapeDtypeStruct((GROUPS, LANES), F32),
            jax.ShapeDtypeStruct((GROUPS, LANES), F32),
        ),
        grid=(ROWS // BLOCK,),
        in_specs=[
            whole(own.shape),
            whole(got.shape),
            pl.BlockSpec((BLOCK, PROTOS), lambda i: (i, 0)),
        ],
        out_specs=(whole((GROUPS, LANES)), whole((GROUPS, LANES))),
        scratch_shapes=[pltpu.VMEM((GROUPS, 8, LANES), F32)],
        compiler_params=params(),
        name="column_pass",
    )(own, got, kern)


def row_kernel(mode, weight_ref, mine_ref, theirs_ref, *refs):
    if mode == "lse":
        lse_ref, kern_ref, sums_ref, scale_ref = refs
    elif mode == "loss":
        rows_ref, protos_ref, kern_ref, sums_ref, scale_ref, scores_ref = refs
    else:
        kern_ref, sums_ref, scale_ref = refs
    step = pl.program_id(0)

    @pl.when(step == 0)
    def _():
        scale_ref[...] = 1.0 / (mine_ref[...] + theirs_ref[...])
        if mode == "lse":
            for group in range(GROUPS):
                spread(sums_ref, GROUPS, group, lse_ref[group : group + 1, :])

    if mode == "loss":
        scores_ref[...] = lax.dot_general(
            rows_ref[...], protos_ref[...], TRANS_B, preferred_element_type=F32
        )
    for half in range(HALVES):
        weight = down(weight_ref[pl.ds(step * HALVES + half, 1), :])
        total = jnp.zeros((LANES, LANES), F32)
        crossed = jnp.zeros((LANES, LANES), F32)
        for group in range(GROUPS):
            at = (slice(half * LANES, (half + 1) * LANES), slice(group * LANES, (group + 1) * LANES))
            part = (kern_ref[at].astype(F32) * weight) * scale_ref[group : group + 1, :]
            total += part
            if mode == "loss":
                crossed += part * scores_ref[at]
        spread(sums_ref, 0, step * HALVES + half, along(total))
        if mode == "loss":
            spread(sums_ref, GROUPS, step * HALVES + half, along(crossed) * S_SCALE)


def row_pass(mode, weight, mine, theirs, kern, extra=()):
    vectors = 1 if mode == "plain" else 2
    extra_specs, scratch = [], []
    if mode == "lse":
        extra_specs = [whole((GROUPS, LANES))]
    elif mode == "loss":
        extra_specs = [pl.BlockSpec((BLOCK, D), lambda i: (i, 0)), whole((PROTOS, D))]
        scratch = [pltpu.VMEM((BLOCK, PROTOS), F32)]
    return pl.pallas_call(
        functools.partial(row_kernel, mode),
        out_shape=(
            jax.ShapeDtypeStruct((PEERS, vectors * GROUPS, LANES), F32),
            jax.ShapeDtypeStruct((GROUPS, LANES), F32),
        ),
        grid=(ROWS // BLOCK,),
        in_specs=[whole((GROUPS, LANES))] * 3
        + extra_specs
        + [pl.BlockSpec((BLOCK, PROTOS), lambda i: (i, 0))],
        out_specs=(whole((PEERS, vectors * GROUPS, LANES)), whole((GROUPS, LANES))),
        scratch_shapes=scratch,
        compiler_params=params(),
        name="row_pass",
    )(weight, mine, theirs, *extra, kern)


def grad_kernel(
    core, weight_ref, got_ref, lses_ref, scale_ref, kern_ref, rows_ref, protos_ref,
    student_ref, keep_ref, send_ref, loss_ref, scaled_ref, lse_ref, scores_ref, logits_ref, acc_ref,
):
    step = pl.program_id(0)

    @pl.when(step == 0)
    def _():
        sums = jnp.sum(got_ref[:, :GROUPS, :], axis=0)
        crossed = jnp.sum(got_ref[:, GROUPS:, :], axis=0)
        top = lses_ref[0]
        for peer in range(1, PEERS):
            top = jnp.maximum(top, lses_ref[peer])
        total = jnp.zeros_like(top)
        for peer in range(PEERS):
            total += jnp.exp(lses_ref[peer] - top)
        lse = top + jnp.log(total)
        lse_ref[...] = lse
        scaled_ref[...] = weight_ref[...] / sums
        terms = (lse * sums - crossed) / sums
        terms = jnp.sum(jnp.sum(terms, axis=0, keepdims=True), axis=1, keepdims=True)
        loss_ref[...] = jnp.broadcast_to(terms, (8, LANES))
        acc_ref[...] = jnp.zeros_like(acc_ref)

    rows = rows_ref[...]
    scores_ref[...] = lax.dot_general(rows, protos_ref[...], TRANS_B, preferred_element_type=F32)
    for half in range(HALVES):
        weight = down(scaled_ref[pl.ds(step * HALVES + half, 1), :])
        lse = down(lse_ref[pl.ds(step * HALVES + half, 1), :])
        for group in range(GROUPS):
            at = (slice(half * LANES, (half + 1) * LANES), slice(group * LANES, (group + 1) * LANES))
            target = (kern_ref[at].astype(F32) * weight) * scale_ref[group : group + 1, :]
            prob = jnp.exp(scores_ref[at] * S_SCALE - lse)
            logits_ref[at] = ((prob - target) * (1.0 / (0.1 * TOTAL_ROWS))).astype(BF16)
    logits = logits_ref[...]
    student_ref[...] = jnp.dot(logits, protos_ref[...], preferred_element_type=F32).astype(BF16)
    acc_ref[...] += jnp.dot(jnp.transpose(rows), logits, preferred_element_type=F32)

    @pl.when(step == pl.num_programs(0) - 1)
    def _():
        for z in range(Z):
            for c in range(C):
                first = (z * C + c) * OWN_PROTOS
                part = jnp.transpose(acc_ref[:, first : first + OWN_PROTOS])

                @pl.when(core[0] == c)
                def _(part=part, z=z):
                    keep_ref[z] = part

                @pl.when(core[0] != c)
                def _(part=part, z=z):
                    send_ref[z] = part.astype(BF16)


def gradients(core, weight, got, lses, scale, kern, rows, protos):
    return pl.pallas_call(
        grad_kernel,
        out_shape=(
            jax.ShapeDtypeStruct((ROWS, D), BF16),
            jax.ShapeDtypeStruct((Z, OWN_PROTOS, D), F32),
            jax.ShapeDtypeStruct((Z, OWN_PROTOS, D), BF16),
            jax.ShapeDtypeStruct((8, LANES), F32),
        ),
        grid_spec=pltpu.PrefetchScalarGridSpec(
            num_scalar_prefetch=1,
            grid=(ROWS // BLOCK,),
            in_specs=[
                whole(weight.shape),
                whole(got.shape),
                whole(lses.shape),
                whole(scale.shape),
                pl.BlockSpec((BLOCK, PROTOS), lambda i, *_: (i, 0)),
                pl.BlockSpec((BLOCK, D), lambda i, *_: (i, 0)),
                whole((PROTOS, D)),
            ],
            out_specs=(
                pl.BlockSpec((BLOCK, D), lambda i, *_: (i, 0)),
                whole((Z, OWN_PROTOS, D)),
                whole((Z, OWN_PROTOS, D)),
                whole((8, LANES)),
            ),
            scratch_shapes=[
                pltpu.VMEM((GROUPS, LANES), F32),
                pltpu.VMEM((GROUPS, LANES), F32),
                pltpu.VMEM((BLOCK, PROTOS), F32),
                pltpu.VMEM((BLOCK, PROTOS), BF16),
                pltpu.VMEM((D, PROTOS), F32),
            ],
        ),
        compiler_params=params(),
        name="gradients",
    )(core, weight, got, lses, scale, kern, rows, protos)


TAIL = 16


def split_kernel(zs, keep_ref, got_ref, loss_ref, other_ref, mine_ref, *outs):
    step = pl.program_id(0)
    part = keep_ref[0] + got_ref[0].astype(F32)
    value = jnp.broadcast_to((loss_ref[...] + other_ref[...])[0:1, :], (TAIL, LANES))
    high = value.astype(BF16)
    rest = value - high.astype(F32)
    middle = rest.astype(BF16)
    low = (rest - middle.astype(F32)).astype(BF16)
    row = lax.broadcasted_iota(jnp.int32, (TAIL, LANES), 0)
    tail = jnp.where(row == 0, high.astype(F32), jnp.where(row == 1, middle.astype(F32), low.astype(F32)))
    tail = jnp.concatenate([tail, tail], axis=1).astype(BF16)
    for shift in range(Z):
        @pl.when(step == shift)
        def _(shift=shift):
            if shift == 0:
                mine_ref[...] = part
            else:
                outs[shift][:OWN_PROTOS, :] = part.astype(BF16)
            outs[shift][OWN_PROTOS:, :] = tail


def split_sums(zs, keep, got, loss, other):
    return pl.pallas_call(
        split_kernel,
        out_shape=(jax.ShapeDtypeStruct((OWN_PROTOS, D), F32),)
        + (jax.ShapeDtypeStruct((OWN_PROTOS + TAIL, D), BF16),) * Z,
        grid_spec=pltpu.PrefetchScalarGridSpec(
            num_scalar_prefetch=1,
            grid=(Z,),
            in_specs=[
                pl.BlockSpec((1, OWN_PROTOS, D), lambda i, zs: (zs[i], 0, 0)),
                pl.BlockSpec((1, OWN_PROTOS, D), lambda i, zs: (zs[i], 0, 0)),
                whole((8, LANES)),
                whole((8, LANES)),
            ],
            out_specs=(whole((OWN_PROTOS, D)),) + (whole((OWN_PROTOS + TAIL, D)),) * Z,
        ),
        compiler_params=params(),
        name="split_sums",
    )(zs, keep, got, loss, other)


def join_kernel(zfrom, mine_ref, *refs):
    parts, (out_ref, loss_ref, value_ref) = refs[:Z], refs[Z:]
    total = mine_ref[...]
    for shift, part in enumerate(parts):
        if shift:
            total += part[:OWN_PROTOS, :].astype(F32)
        tail = part[OWN_PROTOS:, :LANES].astype(F32)
        value_ref[pl.ds(zfrom[shift], 1), :] = tail[0:1] + (tail[1:2] + tail[2:3])
    out_ref[...] = total
    loss = value_ref[0:1, :]
    for z in range(1, Z):
        loss = loss + value_ref[z : z + 1, :]
    loss_ref[...] = jnp.broadcast_to(loss, (8, LANES)) * (1.0 / TOTAL_ROWS)


def join_sums(zfrom, mine, parts):
    return pl.pallas_call(
        join_kernel,
        out_shape=(jax.ShapeDtypeStruct((OWN_PROTOS, D), F32), jax.ShapeDtypeStruct((8, LANES), F32)),
        grid_spec=pltpu.PrefetchScalarGridSpec(
            num_scalar_prefetch=1,
            grid=(1,),
            in_specs=[whole(mine.shape)] + [whole(p.shape) for p in parts],
            out_specs=(whole((OWN_PROTOS, D)), whole((8, LANES))),
            scratch_shapes=[pltpu.VMEM((Z, LANES), F32)],
        ),
        compiler_params=params(),
        name="join_sums",
    )(zfrom, mine, *parts)


def shift_x(value, by):
    return lax.ppermute(value, "x", [(i, (i + by) % X) for i in range(X)])


def shift_z(value, by):
    return lax.ppermute(value, "z", [(i, (i + by) % Z) for i in range(Z)])


def swap_core(value):
    return lax.ppermute(value, "c", [(0, 1), (1, 0)])


def share_z(value):
    got = {}
    for by in (4, 3, 2, 1):
        pairs = [(z * C + 1, (z - by) % Z * C + 1) for z in range(Z)]
        if by < 4:
            pairs += [(z * C, (z + by) % Z * C) for z in range(Z)]
        got[by] = lax.ppermute(value, ("z", "c"), pairs)
    return [got[by] for by in (1, 2, 3, 4)]


def column_total(sums, core):
    chip = sums + swap_core(sums)
    got = share_z(chip)
    part = jnp.where(core == 0, chip, 0.0) + ((got[0] + got[1]) + (got[2] + got[3]))
    return part, swap_core(part)


def exchange(parts):
    return lax.all_to_all(parts, ("x", "y"), 0, 0, tiled=True)


def body(teacher_tokens, student_tokens, masked_index, prototypes):
    x, z, core = lax.axis_index("x"), lax.axis_index("z"), lax.axis_index("c")
    xpos = jnp.stack([x, (x + 3) % X, (x + 1) % X, (x + 2) % X]).astype(jnp.int32)
    before = [(z + Z - k) % Z for k in (1, 2, 3)]
    after = [(z + k) % Z for k in (1, 2, 3)]
    far = (z + 4) % Z
    first = [jnp.where(core == 0, b, a) for b, a in zip(before, after)]
    second = [jnp.where(core == 0, a, b) for b, a in zip(before, after)]
    wpos = jnp.stack([z, *first, far, *second, far]).astype(jnp.int32)
    one = jnp.ones((), jnp.int32)
    wvalid = jnp.stack([one] * 4 + [core] + [one] * 3 + [1 - core]).astype(jnp.int32)
    zs = ((z + jnp.arange(Z)) % Z).astype(jnp.int32)
    zfrom = ((z + Z - jnp.arange(Z)) % Z).astype(jnp.int32)
    cores = core[None].astype(jnp.int32)

    other = swap_core(prototypes)
    chip_protos = jnp.where(
        core == 0,
        jnp.concatenate([prototypes, other], axis=0),
        jnp.concatenate([other, prototypes], axis=0),
    )
    from_z = share_z(chip_protos)
    from_core = [swap_core(part) for part in from_z]
    protos_in = [chip_protos, *from_z, *from_core]
    teacher_rows = pick_rows(masked_index, teacher_tokens)
    teacher_in = [teacher_rows] + [shift_x(teacher_rows, by) for by in (1, -1, 2)]
    student_rows = pick_rows(masked_index, student_tokens)
    student_in = [student_rows] + [shift_x(student_rows, by) for by in (1, -1, 2)]

    kern, top, tops, protos = teacher_scores(xpos, wpos, wvalid, teacher_in, protos_in)
    sums, weight = column_pass(True, top, exchange(tops), kern)
    rows, lse = student_totals(xpos, student_in, protos)
    mine, theirs = column_total(sums, core)
    got, _ = row_pass("plain", weight, mine, theirs, kern)
    sums, _ = column_pass(False, weight, exchange(got), kern)
    mine, theirs = column_total(sums, core)
    got, _ = row_pass("lse", weight, mine, theirs, kern, (lse,))
    got = exchange(got)
    lses = got[:, GROUPS:, :]
    sums, _ = column_pass(False, weight, got, kern)
    mine, theirs = column_total(sums, core)
    got, scale = row_pass("loss", weight, mine, theirs, kern, (rows, protos))
    got = exchange(got)
    student, keep, send, loss = gradients(cores, weight, got, lses, scale, kern, rows, protos)

    mine, own, *sends = split_sums(zs, keep, swap_core(send), loss, swap_core(loss))
    parts = [own] + [shift_z(part, by) for by, part in enumerate(sends, 1)]
    student = exchange(student.reshape(PEERS, ROWS // PEERS, D))
    student = jnp.sum(student.astype(F32), axis=0).astype(BF16)
    student = lax.all_to_all(
        jnp.broadcast_to(student[None], (Y,) + student.shape), "y", 0, 0, tiled=True
    )
    grad_weight, loss = join_sums(zfrom, mine, parts)
    return loss[0, 0], student.reshape(OWN_ROWS, D), grad_weight


def solution(mesh):
    named = Mesh(mesh.devices.reshape(X, Z, C, Y), ("x", "z", "c", "y"))
    batch = ("x", "z", "c")
    placed = (
        P(batch, None, None),
        P(batch, None, None),
        P(batch, None),
        P((*batch, "y"), None),
    )
    return jax.shard_map(
        body,
        mesh=named,
        in_specs=placed,
        out_specs=(P(), P(batch, None), P((*batch, "y"), None)),
        check_vma=False,
    )
```

time: 1130 us -> 238 us (0.21)
  blocking collectives: 876 us -> 25.1 us
  starting transfers between devices: 0.08 us -> 87.6 us
  other arithmetic: 80 us -> 1.22 us
  waiting for transfers between devices: 117 us -> 52.9 us
  Pallas kernels: 0 us -> 55.2 us
  matrix products: 28.1 us -> 0 us
  between operations: 16.5 us -> 0.9 us
    psum x8 -> x0, blocking collectives: 858 us -> none  [the longest x3 739 us: column_scale(): return 1.0 / lax.psum(partial_value, 'batch')]
    all_gather x1 -> x0, waiting for transfers between devices: 72.9 us -> none  [body(): gathered = lax.all_gather(prototypes, 'batch', axis=0, tiled=True)]
    ppermute x0 -> x42, starting transfers between devices: none -> 67.4 us  [the longest x16 26.3 us: share_z(): got[by] = lax.ppermute(value, ('z', 'c'), pairs)]
    reduce_sum x6 -> x1, other arithmetic: 56.1 us -> 0.14 us  [body(): student = jnp.sum(student.astype(F32), axis=0).astype(BF16)]
    pallas_call x0 -> x13, Pallas kernels: none -> 55.2 us  [the longest x3 14.3 us: row_pass(): pl.pallas_call(functools.partial(row_kernel, mode), out_shape=(jax.ShapeD...]
    reduce_scatter x1 -> x0, waiting for transfers between devices: 43.3 us -> none  [body(): lax.psum_scatter(lax.dot_general(grad_logits, student_rows, (((0,), (0,))...]
    ppermute x0 -> x42, waiting for transfers between devices: none -> 28.6 us  [the longest x16 16.1 us: share_z(): got[by] = lax.ppermute(value, ('z', 'c'), pairs)]
    dot_general x3 -> x0, matrix products: 28.1 us -> none  [the longest x1 15.6 us: body(): lax.dot_general(stacked, gathered, contract, preferred_element_type=jnp.f...]
  transfers between devices with their start and end apart: 2 -> 46, of which waited for: 2 -> 24; matrix products, arithmetic and copies ran while one was open for 2% -> 1% of each run, Pallas kernels for 0% -> 6%
where the time goes in v1:
time: 238 us; the launch traced here: 237 us
  starting transfers between devices  87.6 us (37%)
  Pallas kernels  55.2 us (23%)
  waiting for transfers between devices  52.9 us (22%)
  blocking collectives  25.1 us (11%)
  local copies, waits for them, and re-layouts  14 us (6%)
    ppermute x16, starting transfers between devices, share_z(): got[by] = lax.ppermute(value, ('z', 'c'), pairs)  26.3 us
    all_to_all x2, blocking collectives, exchange(): return lax.all_to_all(parts, ('x', 'y'), 0, 0, tiled=True)  25.1 us
    all_to_all x3, waiting for transfers between devices, exchange(): return lax.all_to_all(parts, ('x', 'y'), 0, 0, tiled=True)  24.3 us
    ppermute x13, starting transfers between devices, swap_core(): return lax.ppermute(value, 'c', [(0, 1), (1, 0)])  16.5 us
    ppermute x16, waiting for transfers between devices, share_z(): got[by] = lax.ppermute(value, ('z', 'c'), pairs)  16.1 us
    all_to_all x3, starting transfers between devices, exchange(): return lax.all_to_all(parts, ('x', 'y'), 0, 0, tiled=True)  15.3 us
    pallas_call x3, Pallas kernels, row_pass(): pl.pallas_call(functools.partial(row_kernel, mode), out_shape=(jax.ShapeD...  14.3 us
    pallas_call x1, Pallas kernels, gradients(): pl.pallas_call(grad_kernel, out_shape=(jax.ShapeDtypeStruct((ROWS, D), BF...  14.2 us
  transfers between devices with their start and end apart: 46, of which 24 were waited for; matrix products, arithmetic and copies ran while one was open for 1% of the time, Pallas kernels for 6%

profile of v1, /device:TPU:8, one launch (start us, length us, event | category | flops | bytes accessed | tf_op | source)
XLA Modules:
  0.0 236.9 jit_solution(13513739084661755879)
XLA Ops:
  3.1 4.7 %collective-permute-start.6 = (bf16[256,256]{1,0:T(8,128)(2,1)S(1)}, bf16[256,256]{1,0:T(8,128)(2,1)S(1)}, u32[]{:S(2)}, u32[]{:S(2)}) collective-permute-start(bf16[256,256]{1,0:T(8,128)(2,1)S(1)} %maximum_select_fusion.refs_4_), channel_id=1, source_target_pairs={{4,44},{12,52},{20,60},{28,4},{36,12},{44,20},{52,28},{60,36},{0,2... | collective-permute-start | bytes 393224 | tf_op jit(solution)/shard_map/ppermute | solution.py:467
  14.1 3.1 %collective-permute-start.4 = (bf16[256,256]{1,0:T(8,128)(2,1)S(1)}, bf16[256,256]{1,0:T(8,128)(2,1)S(1)}, u32[]{:S(2)}, u32[]{:S(2)}) collective-permute-start(bf16[256,256]{1,0:T(8,128)(2,1)S(1)} %maximum_select_fusion.refs_4_), channel_id=1, source_target_pairs={{4,60},{12,4},{20,12},{28,20},{36,28},{44,36},{52,44},{60,52},{0,8... | collective-permute-start | bytes 393224 | tf_op jit(solution)/shard_map/ppermute | solution.py:467
  21.5 4.5 %collective-permute-start.10 = (bf16[256,256]{1,0:T(8,128)(2,1)S(1)}, bf16[256,256]{1,0:T(8,128)(2,1)S(1)}, u32[]{:S(2)}, u32[]{:S(2)}) collective-permute-start(bf16[256,256]{1,0:T(8,128)(2,1)S(1)} %collective-permute-done.6.refs_7_), channel_id=1, source_target_pairs={{0,4},{4,0},{1,5},{5,1},{2,6},{6,2},{3,7},{7,3},{8,12},{12,8},{9,1... | collective-permute-start | bytes 393224 | tf_op jit(solution)/shard_map/ppermute | solution.py:458
  28.4 7.3 %teacher_scores.1 = (bf16[2048,2048]{1,0:T(8,128)(2,1)S(1)}, f32[16,128]{1,0:T(8,128)S(1)}, f32[16,16,128]{2,1,0:T(8,128)S(1)}, bf16[2048,256]{1,0:T(8,128)(2,1)S(1)}) custom-call(s32[4]{0:T(128)S(1)} %pad_add_fusion.xpos, s32[9]{0:T(128)S(1)} %stack.63.wpos, s32[9]{0:T(128)S(1)} %stack.65.wvalid, bf16[512,256]{1,0:T(8,128)(2,1)S(1)} %pick_rows.2.refs_0_, ...), custom_call_target="tpu_custom_call" | custom-call | tf_op jit(solution)/shard_map/teacher_scores/pallas_call | solution.py:107
  35.8 13.7 %all_to_all.30.got_ref = f32[16,16,128]{2,1,0:T(8,128)S(1)} all-to-all(f32[16,16,128]{2,1,0:T(8,128)S(1)} %get-tuple-element.33), channel_id=1, replica_groups=mesh['x'=4,'z'=8,'c'=2,'y'=4] {'x','y'}, dimensions={0} | all-to-all | bytes 262144 | tf_op jit(solution)/shard_map/all_to_all | solution.py:479
  53.2 2.4 %collective-permute-start.13 = (f32[16,128]{1,0:T(8,128)S(1)}, f32[16,128]{1,0:T(8,128)S(1)}, u32[]{:S(2)}, u32[]{:S(2)}) collective-permute-start(f32[16,128]{1,0:T(8,128)S(1)} %add.150), channel_id=1, source_target_pairs={{4,60},{12,4},{20,12},{28,20},{36,28},{44,36},{52,44},{60,52},{0,8... | collective-permute-start | bytes 24584 | tf_op jit(solution)/shard_map/ppermute | solution.py:467
  56.7 3.2 %collective-permute-start.15 = (f32[16,128]{1,0:T(8,128)S(1)}, f32[16,128]{1,0:T(8,128)S(1)}, u32[]{:S(2)}, u32[]{:S(2)}) collective-permute-start(f32[16,128]{1,0:T(8,128)S(1)} %add.150), channel_id=1, source_target_pairs={{4,44},{12,52},{20,60},{28,4},{36,12},{44,20},{52,28},{60,36},{0,2... | collective-permute-start | bytes 24584 | tf_op jit(solution)/shard_map/ppermute | solution.py:467
  63.3 4.4 %collective-permute-start.17 = (f32[16,128]{1,0:T(8,128)S(1)}, f32[16,128]{1,0:T(8,128)S(1)}, u32[]{:S(2)}, u32[]{:S(2)}) collective-permute-start(f32[16,128]{1,0:T(8,128)S(1)} %add_add_fusion.2.mine_ref), channel_id=1, source_target_pairs={{0,4},{4,0},{1,5},{5,1},{2,6},{6,2},{3,7},{7,3},{8,12},{12,8},{9,1... | collective-permute-start | bytes 24584 | tf_op jit(solution)/shard_map/ppermute | solution.py:458
  68.6 4.1 %row_pass.3 = (f32[16,16,128]{2,1,0:T(8,128)}, f32[16,128]{1,0:T(8,128)}) custom-call(f32[16,128]{1,0:T(8,128)S(1)} %get-tuple-element.35.weight_ref.own_ref, f32[16,128]{1,0:T(8,128)S(1)} %add_add_fusion.2.mine_ref, f32[16,128]{1,0:T(8,128)S(1)} %collective-permute-done.17.theirs_ref, bf16[2048,2048]{1,0:T(8,128)(2,1)S(1)} %get-tuple-element.34.kern_ref.refs_0_.refs_1_.refs_2_), custom_call_target="tpu_custom_call" | custom-call | tf_op jit(solution)/shard_map/row_pass/pallas_call | solution.py:262
  72.7 5.1 %all-to-all-start.1 = ((f32[16,16,128]{2,1,0:T(8,128)}), f32[16,16,128]{2,1,0:T(8,128)S(1)}, u32[]{:S(2)}, u32[]{:S(2)}) async-start(f32[16,16,128]{2,1,0:T(8,128)} %get-tuple-element.37), calls=%async_computation.1 | async-start | bytes 262144 | tf_op jit(solution)/shard_map/all_to_all | solution.py:479
  84.8 3.4 %copy-done.1 = bf16[2048,2048]{1,0:T(8,128)(2,1)S(1)} copy-done((bf16[2048,2048]{1,0:T(8,128)(2,1)S(1)}, bf16[2048,2048]{1,0:T(8,128)(2,1)}, u32[]{:S(2)}) %copy-start.1) | copy-done | bytes 8388632
  88.2 2.9 %column_pass.4 = (f32[16,128]{1,0:T(8,128)S(1)}, f32[16,128]{1,0:T(8,128)}) custom-call(f32[16,128]{1,0:T(8,128)S(1)} %get-tuple-element.35.weight_ref.own_ref, f32[16,16,128]{2,1,0:T(8,128)S(1)} %all-to-all-done.1.got_ref, bf16[2048,2048]{1,0:T(8,128)(2,1)S(1)} %copy-done.1), custom_call_target="tpu_custom_call" | custom-call | tf_op jit(solution)/shard_map/column_pass/pallas_call | solution.py:200
  94.0 3.2 %collective-permute-done.19 = f32[16,128]{1,0:T(8,128)S(1)} collective-permute-done((f32[16,128]{1,0:T(8,128)S(1)}, f32[16,128]{1,0:T(8,128)S(1)}, u32[]{:S(2)}, u32[]{:S(2)}) %collective-permute-start.19) | collective-permute-done | bytes 8224 | tf_op jit(solution)/shard_map/ppermute | solution.py:467
  99.4 4.5 %collective-permute-done.21 = f32[16,128]{1,0:T(8,128)S(1)} collective-permute-done((f32[16,128]{1,0:T(8,128)S(1)}, f32[16,128]{1,0:T(8,128)S(1)}, u32[]{:S(2)}, u32[]{:S(2)}) %collective-permute-start.21) | collective-permute-done | bytes 8224 | tf_op jit(solution)/shard_map/ppermute | solution.py:467
  105.4 8.2 %student_totals.1 = (bf16[2048,256]{1,0:T(8,128)(2,1)S(1)}, f32[16,128]{1,0:T(8,128)S(1)}) custom-call(s32[4]{0:T(128)S(1)} %pad_add_fusion.xpos, bf16[512,256]{1,0:T(8,128)(2,1)S(1)} %pick_rows.3.refs_0_, bf16[512,256]{1,0:T(8,128)(2,1)S(1)} %collective-permute-done.24.refs_1_, bf16[512,256]{1,0:T(8,128)(2,1)S(1)} %collective-permute-done.25.refs_2_, ...), custom_call_target="tpu_custom_call" | custom-call | tf_op jit(solution)/shard_map/student_totals/pallas_call | solution.py:151
  113.7 4.0 %row_pass.4 = (f32[16,32,128]{2,1,0:T(8,128)S(1)}, f32[16,128]{1,0:T(8,128)}) custom-call(f32[16,128]{1,0:T(8,128)S(1)} %get-tuple-element.35.weight_ref.own_ref, f32[16,128]{1,0:T(8,128)S(1)} %add_add_fusion.1.mine_ref, f32[16,128]{1,0:T(8,128)S(1)} %collective-permute-done.23.theirs_ref, f32[16,128]{1,0:T(8,128)S(1)} %get-tuple-element.40.refs_0_, ...), custom_call_target="tpu_custom_call" | custom-call | tf_op jit(solution)/shard_map/row_pass/pallas_call | solution.py:262
  117.7 11.5 %all_to_all.31.got_ref = f32[16,32,128]{2,1,0:T(8,128)S(1)} all-to-all(f32[16,32,128]{2,1,0:T(8,128)S(1)} %get-tuple-element.41), channel_id=1, replica_groups=mesh['x'=4,'z'=8,'c'=2,'y'=4] {'x','y'}, dimensions={0} | all-to-all | bytes 524288 | tf_op jit(solution)/shard_map/all_to_all | solution.py:479
  129.1 2.9 %column_pass.5 = (f32[16,128]{1,0:T(8,128)S(1)}, f32[16,128]{1,0:T(8,128)}) custom-call(f32[16,128]{1,0:T(8,128)S(1)} %get-tuple-element.35.weight_ref.own_ref, f32[16,32,128]{2,1,0:T(8,128)S(1)} %all_to_all.31.got_ref, bf16[2048,2048]{1,0:T(8,128)(2,1)S(1)} %copy-done.2), custom_call_target="tpu_custom_call" | custom-call | tf_op jit(solution)/shard_map/column_pass/pallas_call | solution.py:200
  133.7 2.6 %collective-permute-start.29 = (f32[16,128]{1,0:T(8,128)S(1)}, f32[16,128]{1,0:T(8,128)S(1)}, u32[]{:S(2)}, u32[]{:S(2)}) collective-permute-start(f32[16,128]{1,0:T(8,128)S(1)} %add.160), channel_id=1, source_target_pairs={{4,52},{12,60},{20,4},{28,12},{36,20},{44,28},{52,36},{60,44},{0,1... | collective-permute-start | bytes 24584 | tf_op jit(solution)/shard_map/ppermute | solution.py:467
  139.5 3.5 %collective-permute-done.30 = f32[16,128]{1,0:T(8,128)S(1)} collective-permute-done((f32[16,128]{1,0:T(8,128)S(1)}, f32[16,128]{1,0:T(8,128)S(1)}, u32[]{:S(2)}, u32[]{:S(2)}) %collective-permute-start.30) | collective-permute-done | bytes 8224 | tf_op jit(solution)/shard_map/ppermute | solution.py:467
  143.0 4.2 %collective-permute-start.32 = (f32[16,128]{1,0:T(8,128)S(1)}, f32[16,128]{1,0:T(8,128)S(1)}, u32[]{:S(2)}, u32[]{:S(2)}) collective-permute-start(f32[16,128]{1,0:T(8,128)S(1)} %add_add_fusion.mine_ref), channel_id=1, source_target_pairs={{0,4},{4,0},{1,5},{5,1},{2,6},{6,2},{3,7},{7,3},{8,12},{12,8},{9,1... | collective-permute-start | bytes 24584 | tf_op jit(solution)/shard_map/ppermute | solution.py:458
  148.0 6.1 %row_pass.5 = (f32[16,32,128]{2,1,0:T(8,128)}, f32[16,128]{1,0:T(8,128)S(1)}) custom-call(f32[16,128]{1,0:T(8,128)S(1)} %get-tuple-element.35.weight_ref.own_ref, f32[16,128]{1,0:T(8,128)S(1)} %add_add_fusion.mine_ref, f32[16,128]{1,0:T(8,128)S(1)} %collective-permute-done.32.theirs_ref, bf16[2048,256]{1,0:T(8,128)(2,1)S(1)} %get-tuple-element.43.refs_0_.rows_ref, ...), custom_call_target="tpu_custom_call" | custom-call | tf_op jit(solution)/shard_map/row_pass/pallas_call | solution.py:262
  154.2 5.1 %all-to-all-start.3 = ((f32[16,32,128]{2,1,0:T(8,128)}), f32[16,32,128]{2,1,0:T(8,128)S(1)}, u32[]{:S(2)}, u32[]{:S(2)}) async-start(f32[16,32,128]{2,1,0:T(8,128)} %get-tuple-element.44), calls=%async_computation.3 | async-start | bytes 524288 | tf_op jit(solution)/shard_map/all_to_all | solution.py:479
  159.3 7.6 %all-to-all-done.3.got_ref = f32[16,32,128]{2,1,0:T(8,128)S(1)} async-done(((f32[16,32,128]{2,1,0:T(8,128)}), f32[16,32,128]{2,1,0:T(8,128)S(1)}, u32[]{:S(2)}, u32[]{:S(2)}) %all-to-all-start.3) | async-done | bytes 262176 | tf_op jit(solution)/shard_map/all_to_all | solution.py:479
  166.8 3.4 %copy-done.3 = bf16[2048,2048]{1,0:T(8,128)(2,1)S(1)} copy-done((bf16[2048,2048]{1,0:T(8,128)(2,1)S(1)}, bf16[2048,2048]{1,0:T(8,128)(2,1)}, u32[]{:S(2)}) %copy-start.3) | copy-done | bytes 8388632
  170.2 14.2 %gradients.1 = (bf16[2048,256]{1,0:T(8,128)(2,1)S(1)}, f32[8,128,256]{2,1,0:T(8,128)S(1)}, bf16[8,128,256]{2,1,0:T(8,128)(2,1)S(1)}, f32[8,128]{1,0:T(8,128)S(1)}) custom-call(s32[1]{0:T(128)} %bitcast.core, f32[16,128]{1,0:T(8,128)S(1)} %get-tuple-element.35.weight_ref.own_ref, f32[16,32,128]{2,1,0:T(8,128)S(1)} %all-to-all-done.3.got_ref, ...), custom_call_target="tpu_custom_call" | custom-call | tf_op jit(solution)/shard_map/gradients/pallas_call | solution.py:334
  186.5 5.2 %all-to-all-start.4 = ((bf16[16,128,256]{2,1,0:T(8,128)(2,1)}), bf16[16,128,256]{2,1,0:T(8,128)(2,1)S(1)}, u32[]{:S(2)}, u32[]{:S(2)}) async-start(bf16[16,128,256]{2,1,0:T(8,128)(2,1)} %bitcast.17), calls=%async_computation.4 | async-start | bytes 2097152 | tf_op jit(solution)/shard_map/all_to_all | solution.py:479
  192.1 15.1 %all-to-all-done.4 = bf16[16,128,256]{2,1,0:T(8,128)(2,1)S(1)} async-done(((bf16[16,128,256]{2,1,0:T(8,128)(2,1)}), bf16[16,128,256]{2,1,0:T(8,128)(2,1)S(1)}, u32[]{:S(2)}, u32[]{:S(2)}) %all-to-all-start.4) | async-done | bytes 1048608 | tf_op jit(solution)/shard_map/all_to_all | solution.py:479
  208.1 4.8 %all-to-all-start.5 = ((bf16[4,128,256]{2,1,0:T(8,128)(2,1)}), bf16[4,128,256]{2,1,0:T(8,128)(2,1)S(1)}, u32[]{:S(2)}, u32[]{:S(2)}) async-start(bf16[4,128,256]{2,1,0:T(8,128)(2,1)} %broadcast_in_dim.17), calls=%async_computation.5 | async-start | bytes 524288 | tf_op jit(solution)/shard_map/all_to_all | solution.py:531
  219.0 3.2 %collective-permute-start.38 = (bf16[144,256]{1,0:T(8,128)(2,1)S(1)}, bf16[144,256]{1,0:T(8,128)(2,1)S(1)}, u32[]{:S(2)}, u32[]{:S(2)}) collective-permute-start(bf16[144,256]{1,0:T(8,128)(2,1)S(1)} %get-tuple-element.54), channel_id=1, source_target_pairs={{0,32},{8,40},{16,48},{24,56},{32,0},{40,8},{48,16},{56,24},{1,33}... | collective-permute-start | bytes 221192 | tf_op jit(solution)/shard_map/ppermute | solution.py:454
  224.5 3.2 %collective-permute-start.40 = (bf16[144,256]{1,0:T(8,128)(2,1)S(1)}, bf16[144,256]{1,0:T(8,128)(2,1)S(1)}, u32[]{:S(2)}, u32[]{:S(2)}) collective-permute-start(bf16[144,256]{1,0:T(8,128)(2,1)S(1)} %get-tuple-element.56), channel_id=1, source_target_pairs={{0,48},{8,56},{16,0},{24,8},{32,16},{40,24},{48,32},{56,40},{1,49}... | collective-permute-start | bytes 221192 | tf_op jit(solution)/shard_map/ppermute | solution.py:454
  229.3 3.0 %collective-permute-done.39.refs_5_ = bf16[144,256]{1,0:T(8,128)(2,1)S(1)} collective-permute-done((bf16[144,256]{1,0:T(8,128)(2,1)S(1)}, bf16[144,256]{1,0:T(8,128)(2,1)S(1)}, u32[]{:S(2)}, u32[]{:S(2)}) %collective-permute-start.39) | collective-permute-done | bytes 73760 | tf_op jit(solution)/shard_map/ppermute | solution.py:454
  (116 shorter events, 61.7 us)
Async XLA Ops:
  3.1 14.1 %collective-permute-start.6 = (bf16[256,256]{1,0:T(8,128)(2,1)S(1)}, bf16[256,256]{1,0:T(8,128)(2,1)S(1)}, u32[]{:S(2)}, u32[]{:S(2)}) collective-permute-start(bf16[256,256]{1,0:T(8,128)(2,1)S(1)} %maximum_select_fusion.refs_4_), channel_id=1, source_target_pairs={{4,44},{12,52},{20,60},{28,4},{36,12},{44,20},{52,28},{60,36},{0,2... | collective-permute-start | bytes 393224 | tf_op jit(solution)/shard_map/ppermute | solution.py:467
  7.8 10.9 %collective-permute-start.7 = (bf16[256,256]{1,0:T(8,128)(2,1)S(1)}, bf16[256,256]{1,0:T(8,128)(2,1)S(1)}, u32[]{:S(2)}, u32[]{:S(2)}) collective-permute-start(bf16[256,256]{1,0:T(8,128)(2,1)S(1)} %maximum_select_fusion.refs_4_), channel_id=1, source_target_pairs={{4,36},{12,44},{20,52},{28,60},{36,4},{44,12},{52,20},{60,28},{5,3... | collective-permute-start | bytes 393224 | tf_op jit(solution)/shard_map/ppermute | solution.py:467
  10.8 15.8 %collective-permute-start = (bf16[512,256]{1,0:T(8,128)(2,1)S(1)}, bf16[512,256]{1,0:T(8,128)(2,1)S(1)}, u32[]{:S(2)}, u32[]{:S(2)}) collective-permute-start(bf16[512,256]{1,0:T(8,128)(2,1)S(1)} %pick_rows.2.refs_0_), channel_id=1, source_target_pairs={{0,64},{64,128},{128,192},{192,0},{1,65},{65,129},{129,193},{193,1... | collective-permute-start | bytes 786440 | tf_op jit(solution)/shard_map/ppermute | solution.py:450
  12.3 14.7 %collective-permute-start.1 = (bf16[512,256]{1,0:T(8,128)(2,1)S(1)}, bf16[512,256]{1,0:T(8,128)(2,1)S(1)}, u32[]{:S(2)}, u32[]{:S(2)}) collective-permute-start(bf16[512,256]{1,0:T(8,128)(2,1)S(1)} %pick_rows.2.refs_0_), channel_id=1, source_target_pairs={{0,192},{64,0},{128,64},{192,128},{1,193},{65,1},{129,65},{193,129... | collective-permute-start | bytes 786440 | tf_op jit(solution)/shard_map/ppermute | solution.py:450
  14.1 7.4 %collective-permute-start.4 = (bf16[256,256]{1,0:T(8,128)(2,1)S(1)}, bf16[256,256]{1,0:T(8,128)(2,1)S(1)}, u32[]{:S(2)}, u32[]{:S(2)}) collective-permute-start(bf16[256,256]{1,0:T(8,128)(2,1)S(1)} %maximum_select_fusion.refs_4_), channel_id=1, source_target_pairs={{4,60},{12,4},{20,12},{28,20},{36,28},{44,36},{52,44},{60,52},{0,8... | collective-permute-start | bytes 393224 | tf_op jit(solution)/shard_map/ppermute | solution.py:467
  17.2 9.3 %collective-permute-start.5 = (bf16[256,256]{1,0:T(8,128)(2,1)S(1)}, bf16[256,256]{1,0:T(8,128)(2,1)S(1)}, u32[]{:S(2)}, u32[]{:S(2)}) collective-permute-start(bf16[256,256]{1,0:T(8,128)(2,1)S(1)} %maximum_select_fusion.refs_4_), channel_id=1, source_target_pairs={{4,52},{12,60},{20,4},{28,12},{36,20},{44,28},{52,36},{60,44},{0,1... | collective-permute-start | bytes 393224 | tf_op jit(solution)/shard_map/ppermute | solution.py:467
  18.7 8.7 %collective-permute-start.2 = (bf16[512,256]{1,0:T(8,128)(2,1)S(1)}, bf16[512,256]{1,0:T(8,128)(2,1)S(1)}, u32[]{:S(2)}, u32[]{:S(2)}) collective-permute-start(bf16[512,256]{1,0:T(8,128)(2,1)S(1)} %pick_rows.2.refs_0_), channel_id=1, source_target_pairs={{0,128},{64,192},{128,0},{192,64},{1,129},{65,193},{129,1},{193,65... | collective-permute-start | bytes 786440 | tf_op jit(solution)/shard_map/ppermute | solution.py:450
  21.5 5.9 %collective-permute-start.10 = (bf16[256,256]{1,0:T(8,128)(2,1)S(1)}, bf16[256,256]{1,0:T(8,128)(2,1)S(1)}, u32[]{:S(2)}, u32[]{:S(2)}) collective-permute-start(bf16[256,256]{1,0:T(8,128)(2,1)S(1)} %collective-permute-done.6.refs_7_), channel_id=1, source_target_pairs={{0,4},{4,0},{1,5},{5,1},{2,6},{6,2},{3,7},{7,3},{8,12},{12,8},{9,1... | collective-permute-start | bytes 393224 | tf_op jit(solution)/shard_map/ppermute | solution.py:458
  53.2 7.5 %collective-permute-start.13 = (f32[16,128]{1,0:T(8,128)S(1)}, f32[16,128]{1,0:T(8,128)S(1)}, u32[]{:S(2)}, u32[]{:S(2)}) collective-permute-start(f32[16,128]{1,0:T(8,128)S(1)} %add.150), channel_id=1, source_target_pairs={{4,60},{12,4},{20,12},{28,20},{36,28},{44,36},{52,44},{60,52},{0,8... | collective-permute-start | bytes 24584 | tf_op jit(solution)/shard_map/ppermute | solution.py:467
  55.6 5.8 %collective-permute-start.14 = (f32[16,128]{1,0:T(8,128)S(1)}, f32[16,128]{1,0:T(8,128)S(1)}, u32[]{:S(2)}, u32[]{:S(2)}) collective-permute-start(f32[16,128]{1,0:T(8,128)S(1)} %add.150), channel_id=1, source_target_pairs={{4,52},{12,60},{20,4},{28,12},{36,20},{44,28},{52,36},{60,44},{0,1... | collective-permute-start | bytes 24584 | tf_op jit(solution)/shard_map/ppermute | solution.py:467
  56.7 6.7 %collective-permute-start.15 = (f32[16,128]{1,0:T(8,128)S(1)}, f32[16,128]{1,0:T(8,128)S(1)}, u32[]{:S(2)}, u32[]{:S(2)}) collective-permute-start(f32[16,128]{1,0:T(8,128)S(1)} %add.150), channel_id=1, source_target_pairs={{4,44},{12,52},{20,60},{28,4},{36,12},{44,20},{52,28},{60,36},{0,2... | collective-permute-start | bytes 24584 | tf_op jit(solution)/shard_map/ppermute | solution.py:467
  72.7 12.1 %all-to-all-start.1 = ((f32[16,16,128]{2,1,0:T(8,128)}), f32[16,16,128]{2,1,0:T(8,128)S(1)}, u32[]{:S(2)}, u32[]{:S(2)}) async-start(f32[16,16,128]{2,1,0:T(8,128)} %get-tuple-element.37), calls=%async_computation.1 | async-start | bytes 262144 | tf_op jit(solution)/shard_map/all_to_all | solution.py:479
  78.1 27.3 %collective-permute-start.24 = (bf16[512,256]{1,0:T(8,128)(2,1)S(1)}, bf16[512,256]{1,0:T(8,128)(2,1)S(1)}, u32[]{:S(2)}, u32[]{:S(2)}) collective-permute-start(bf16[512,256]{1,0:T(8,128)(2,1)S(1)} %pick_rows.3.refs_0_), channel_id=1, source_target_pairs={{0,64},{64,128},{128,192},{192,0},{1,65},{65,129},{129,193},{193,1... | collective-permute-start | bytes 786440 | tf_op jit(solution)/shard_map/ppermute | solution.py:450
  79.6 25.8 %collective-permute-start.25 = (bf16[512,256]{1,0:T(8,128)(2,1)S(1)}, bf16[512,256]{1,0:T(8,128)(2,1)S(1)}, u32[]{:S(2)}, u32[]{:S(2)}) collective-permute-start(bf16[512,256]{1,0:T(8,128)(2,1)S(1)} %pick_rows.3.refs_0_), channel_id=1, source_target_pairs={{0,192},{64,0},{128,64},{192,128},{1,193},{65,1},{129,65},{193,129... | collective-permute-start | bytes 786440 | tf_op jit(solution)/shard_map/ppermute | solution.py:450
  81.4 24.0 %collective-permute-start.26 = (bf16[512,256]{1,0:T(8,128)(2,1)S(1)}, bf16[512,256]{1,0:T(8,128)(2,1)S(1)}, u32[]{:S(2)}, u32[]{:S(2)}) collective-permute-start(bf16[512,256]{1,0:T(8,128)(2,1)S(1)} %pick_rows.3.refs_0_), channel_id=1, source_target_pairs={{0,128},{64,192},{128,0},{192,64},{1,129},{65,193},{129,1},{193,65... | collective-permute-start | bytes 786440 | tf_op jit(solution)/shard_map/ppermute | solution.py:450
  92.9 5.8 %collective-permute-start.20 = (f32[16,128]{1,0:T(8,128)S(1)}, f32[16,128]{1,0:T(8,128)S(1)}, u32[]{:S(2)}, u32[]{:S(2)}) collective-permute-start(f32[16,128]{1,0:T(8,128)S(1)} %add.155), channel_id=1, source_target_pairs={{4,52},{12,60},{20,4},{28,12},{36,20},{44,28},{52,36},{60,44},{0,1... | collective-permute-start | bytes 24584 | tf_op jit(solution)/shard_map/ppermute | solution.py:467
  97.2 6.7 %collective-permute-start.21 = (f32[16,128]{1,0:T(8,128)S(1)}, f32[16,128]{1,0:T(8,128)S(1)}, u32[]{:S(2)}, u32[]{:S(2)}) collective-permute-start(f32[16,128]{1,0:T(8,128)S(1)} %add.155), channel_id=1, source_target_pairs={{4,44},{12,52},{20,60},{28,4},{36,12},{44,20},{52,28},{60,36},{0,2... | collective-permute-start | bytes 24584 | tf_op jit(solution)/shard_map/ppermute | solution.py:467
  103.8 9.8 %collective-permute-start.23 = (f32[16,128]{1,0:T(8,128)S(1)}, f32[16,128]{1,0:T(8,128)S(1)}, u32[]{:S(2)}, u32[]{:S(2)}) collective-permute-start(f32[16,128]{1,0:T(8,128)S(1)} %add_add_fusion.1.mine_ref), channel_id=1, source_target_pairs={{0,4},{4,0},{1,5},{5,1},{2,6},{6,2},{3,7},{7,3},{8,12},{12,8},{9,1... | collective-permute-start | bytes 24584 | tf_op jit(solution)/shard_map/ppermute | solution.py:458
  133.2 6.1 %collective-permute-start.28 = (f32[16,128]{1,0:T(8,128)S(1)}, f32[16,128]{1,0:T(8,128)S(1)}, u32[]{:S(2)}, u32[]{:S(2)}) collective-permute-start(f32[16,128]{1,0:T(8,128)S(1)} %add.160), channel_id=1, source_target_pairs={{4,60},{12,4},{20,12},{28,20},{36,28},{44,36},{52,44},{60,52},{0,8... | collective-permute-start | bytes 24584 | tf_op jit(solution)/shard_map/ppermute | solution.py:467
  136.3 6.7 %collective-permute-start.30 = (f32[16,128]{1,0:T(8,128)S(1)}, f32[16,128]{1,0:T(8,128)S(1)}, u32[]{:S(2)}, u32[]{:S(2)}) collective-permute-start(f32[16,128]{1,0:T(8,128)S(1)} %add.160), channel_id=1, source_target_pairs={{4,44},{12,52},{20,60},{28,4},{36,12},{44,20},{52,28},{60,36},{0,2... | collective-permute-start | bytes 24584 | tf_op jit(solution)/shard_map/ppermute | solution.py:467
  154.2 12.7 %all-to-all-start.3 = ((f32[16,32,128]{2,1,0:T(8,128)}), f32[16,32,128]{2,1,0:T(8,128)S(1)}, u32[]{:S(2)}, u32[]{:S(2)}) async-start(f32[16,32,128]{2,1,0:T(8,128)} %get-tuple-element.44), calls=%async_computation.3 | async-start | bytes 524288 | tf_op jit(solution)/shard_map/all_to_all | solution.py:479
  186.5 20.8 %all-to-all-start.4 = ((bf16[16,128,256]{2,1,0:T(8,128)(2,1)}), bf16[16,128,256]{2,1,0:T(8,128)(2,1)S(1)}, u32[]{:S(2)}, u32[]{:S(2)}) async-start(bf16[16,128,256]{2,1,0:T(8,128)(2,1)} %bitcast.17), calls=%async_computation.4 | async-start | bytes 2097152 | tf_op jit(solution)/shard_map/all_to_all | solution.py:479
  191.6 21.3 %collective-permute-start.33 = (bf16[8,128,256]{2,1,0:T(8,128)(2,1)S(1)}, bf16[8,128,256]{2,1,0:T(8,128)(2,1)S(1)}, u32[]{:S(2)}, u32[]{:S(2)}) collective-permute-start(bf16[8,128,256]{2,1,0:T(8,128)(2,1)S(1)} %get-tuple-element.47), channel_id=1, source_target_pairs={{0,4},{4,0},{1,5},{5,1},{2,6},{6,2},{3,7},{7,3},{8,12},{12,8},{9,1... | collective-permute-start | bytes 1572872 | tf_op jit(solution)/shard_map/ppermute | solution.py:458
  191.6 21.3 %collective-permute-start.34 = (f32[8,128]{1,0:T(8,128)S(1)}, f32[8,128]{1,0:T(8,128)S(1)}, u32[]{:S(2)}, u32[]{:S(2)}) collective-permute-start(f32[8,128]{1,0:T(8,128)S(1)} %get-tuple-element.48.loss_ref), channel_id=1, source_target_pairs={{0,4},{4,0},{1,5},{5,1},{2,6},{6,2},{3,7},{7,3},{8,12},{12,8},{9,1... | collective-permute-start | bytes 12296 | tf_op jit(solution)/shard_map/ppermute | solution.py:458
  208.1 28.1 %all-to-all-start.5 = ((bf16[4,128,256]{2,1,0:T(8,128)(2,1)}), bf16[4,128,256]{2,1,0:T(8,128)(2,1)S(1)}, u32[]{:S(2)}, u32[]{:S(2)}) async-start(bf16[4,128,256]{2,1,0:T(8,128)(2,1)} %broadcast_in_dim.17), calls=%async_computation.5 | async-start | bytes 524288 | tf_op jit(solution)/shard_map/all_to_all | solution.py:531
  215.2 9.2 %collective-permute-start.35 = (bf16[144,256]{1,0:T(8,128)(2,1)S(1)}, bf16[144,256]{1,0:T(8,128)(2,1)S(1)}, u32[]{:S(2)}, u32[]{:S(2)}) collective-permute-start(bf16[144,256]{1,0:T(8,128)(2,1)S(1)} %get-tuple-element.51), channel_id=1, source_target_pairs={{0,8},{8,16},{16,24},{24,32},{32,40},{40,48},{48,56},{56,0},{1,9},... | collective-permute-start | bytes 221192 | tf_op jit(solution)/shard_map/ppermute | solution.py:454
  216.2 11.5 %collective-permute-start.36 = (bf16[144,256]{1,0:T(8,128)(2,1)S(1)}, bf16[144,256]{1,0:T(8,128)(2,1)S(1)}, u32[]{:S(2)}, u32[]{:S(2)}) collective-permute-start(bf16[144,256]{1,0:T(8,128)(2,1)S(1)} %get-tuple-element.52), channel_id=1, source_target_pairs={{0,16},{8,24},{16,32},{24,40},{32,48},{40,56},{48,0},{56,8},{1,17}... | collective-permute-start | bytes 221192 | tf_op jit(solution)/shard_map/ppermute | solution.py:454
  216.6 12.6 %collective-permute-start.37 = (bf16[144,256]{1,0:T(8,128)(2,1)S(1)}, bf16[144,256]{1,0:T(8,128)(2,1)S(1)}, u32[]{:S(2)}, u32[]{:S(2)}) collective-permute-start(bf16[144,256]{1,0:T(8,128)(2,1)S(1)} %get-tuple-element.53), channel_id=1, source_target_pairs={{0,24},{8,32},{16,40},{24,48},{32,56},{40,0},{48,8},{56,16},{1,25}... | collective-permute-start | bytes 221192 | tf_op jit(solution)/shard_map/ppermute | solution.py:454
  219.0 10.3 %collective-permute-start.38 = (bf16[144,256]{1,0:T(8,128)(2,1)S(1)}, bf16[144,256]{1,0:T(8,128)(2,1)S(1)}, u32[]{:S(2)}, u32[]{:S(2)}) collective-permute-start(bf16[144,256]{1,0:T(8,128)(2,1)S(1)} %get-tuple-element.54), channel_id=1, source_target_pairs={{0,32},{8,40},{16,48},{24,56},{32,0},{40,8},{48,16},{56,24},{1,33}... | collective-permute-start | bytes 221192 | tf_op jit(solution)/shard_map/ppermute | solution.py:454
  222.2 10.0 %collective-permute-start.39 = (bf16[144,256]{1,0:T(8,128)(2,1)S(1)}, bf16[144,256]{1,0:T(8,128)(2,1)S(1)}, u32[]{:S(2)}, u32[]{:S(2)}) collective-permute-start(bf16[144,256]{1,0:T(8,128)(2,1)S(1)} %get-tuple-element.55), channel_id=1, source_target_pairs={{0,40},{8,48},{16,56},{24,0},{32,8},{40,16},{48,24},{56,32},{1,41}... | collective-permute-start | bytes 221192 | tf_op jit(solution)/shard_map/ppermute | solution.py:454
  224.5 8.9 %collective-permute-start.40 = (bf16[144,256]{1,0:T(8,128)(2,1)S(1)}, bf16[144,256]{1,0:T(8,128)(2,1)S(1)}, u32[]{:S(2)}, u32[]{:S(2)}) collective-permute-start(bf16[144,256]{1,0:T(8,128)(2,1)S(1)} %get-tuple-element.56), channel_id=1, source_target_pairs={{0,48},{8,56},{16,0},{24,8},{32,16},{40,24},{48,32},{56,40},{1,49}... | collective-permute-start | bytes 221192 | tf_op jit(solution)/shard_map/ppermute | solution.py:454
  227.7 6.7 %collective-permute-start.41 = (bf16[144,256]{1,0:T(8,128)(2,1)S(1)}, bf16[144,256]{1,0:T(8,128)(2,1)S(1)}, u32[]{:S(2)}, u32[]{:S(2)}) collective-permute-start(bf16[144,256]{1,0:T(8,128)(2,1)S(1)} %get-tuple-element.57), channel_id=1, source_target_pairs={{0,56},{8,0},{16,8},{24,16},{32,24},{40,32},{48,40},{56,48},{1,57}... | collective-permute-start | bytes 221192 | tf_op jit(solution)/shard_map/ppermute | solution.py:454
  (25 other events, 174.1 us)

commit v2 on v0

v2 whole, which is shorter than its diff:
```python
import functools
import math

import jax
import jax.numpy as jnp
from jax import lax
from jax.experimental import pallas as pl
from jax.experimental.pallas import tpu as pltpu
from jax.sharding import Mesh, PartitionSpec as P

X, Z, C, Y = 4, 8, 2, 4
F32, BF16 = jnp.float32, jnp.bfloat16
D = 256
IMAGES = 8
MASKED = 64
OWN_ROWS = 512
OWN_PROTOS = 128
ROWS = X * OWN_ROWS
PROTOS = Z * C * OWN_PROTOS
TOTAL_ROWS = ROWS * Z * C
PEERS = X * Y
LANES = 128
GROUPS = 16
BLOCK = 256
HALVES = BLOCK // LANES
T_SCALE = 1.0 / 0.07
S_SCALE = 1.0 / 0.1
MIB = 1 << 20
UNROLL = 16
LOG2E = math.log2(math.e)
GRAD_SCALE = 1.0 / (0.1 * TOTAL_ROWS)
TRANS_B = (((1,), (1,)), ((), ()))


def whole(shape):
    return pl.BlockSpec(shape, lambda *_: (0,) * len(shape))


def params(mib=32):
    return pltpu.CompilerParams(vmem_limit_bytes=mib * MIB)


def in_vmem(array):
    return pltpu.with_memory_space_constraint(array, pltpu.VMEM)


def down(row):
    return jnp.transpose(jnp.broadcast_to(row, (LANES, LANES)))


def along(column_parts):
    return jnp.sum(jnp.transpose(column_parts), axis=0, keepdims=True)


def spread(ref, first, at, row):
    ref[:, pl.ds(first + at, 1), :] = jnp.broadcast_to(row[None], (ref.shape[0], 1, LANES))


def pick_kernel(index_ref, tokens_ref, out_ref):
    for image in range(IMAGES):
        at = lax.broadcasted_iota(jnp.int32, (D, MASKED), 0)
        chosen = (at == index_ref[image : image + 1, :]).astype(BF16)
        rows = lax.dot_general(
            chosen, tokens_ref[image], (((0,), (0,)), ((), ())), preferred_element_type=F32
        )
        out_ref[image * MASKED : (image + 1) * MASKED, :] = rows.astype(BF16)


def pick_rows(index, tokens):
    return pl.pallas_call(
        pick_kernel,
        out_shape=jax.ShapeDtypeStruct((OWN_ROWS, D), BF16),
        in_specs=[whole(index.shape), whole(tokens.shape)],
        out_specs=whole((OWN_ROWS, D)),
        grid=(1,),
        compiler_params=params(),
        name="pick_rows",
    )(index, tokens)


def place_rows(pieces, out_ref):
    x = lax.axis_index("x")
    for piece, by in zip(pieces, (0, 2, 1, -1)):
        at = lax.rem(x + X - by, X) * OWN_ROWS
        out_ref[pl.ds(pl.multiple_of(at, OWN_ROWS), OWN_ROWS), :] = piece[...]


def place_protos(pieces, out_ref):
    z, core = lax.axis_index("z"), lax.axis_index("c")
    sign = 1 - 2 * core
    chips = [(z, core)]
    chips += [(lax.rem(z + Z - sign * by, Z), core) for by in (1, 2, 3)]
    chips += [(lax.rem(z + Z + sign * by, Z), 1 - core) for by in (1, 2, 3)]
    far = lax.rem(z + Z // 2, Z)
    chips += [(far, core), (far, 1 - core)]
    for piece, (chip, first) in zip(pieces, chips):
        for half in range(piece.shape[0] // OWN_PROTOS):
            which = first if half == 0 else 1 - first
            at = pl.multiple_of((chip * C + which) * OWN_PROTOS, OWN_PROTOS)
            out_ref[pl.ds(at, OWN_PROTOS), :] = piece[half * OWN_PROTOS : (half + 1) * OWN_PROTOS, :]


def teacher_kernel(*refs):
    rows_in, protos_in = refs[:X], refs[X : X + 9]
    kern_ref, top_ref, tops_ref, protos_ref, rows_ref = refs[X + 9 :]
    step = pl.program_id(0)

    @pl.when(step == 0)
    def _():
        place_rows(rows_in, rows_ref)
        place_protos(protos_in, protos_ref)

    rows = rows_ref[pl.ds(pl.multiple_of(step * BLOCK, BLOCK), BLOCK), :]
    scores = lax.dot_general(rows, protos_ref[...], TRANS_B, preferred_element_type=F32)
    top = jnp.max(scores, axis=1, keepdims=True)
    kern_ref[...] = jnp.exp2((scores - top) * (T_SCALE * LOG2E)).astype(BF16)
    for half in range(HALVES):
        part = jnp.broadcast_to(top[half * LANES : (half + 1) * LANES], (LANES, LANES))
        row = jnp.transpose(part)[0:1, :] * T_SCALE
        top_ref[pl.ds(step * HALVES + half, 1), :] = row
        spread(tops_ref, 0, step * HALVES + half, row)


def teacher_scores(rows, protos):
    return pl.pallas_call(
        teacher_kernel,
        out_shape=(
            pltpu.VMEM((ROWS, PROTOS), BF16),
            jax.ShapeDtypeStruct((GROUPS, LANES), F32),
            jax.ShapeDtypeStruct((PEERS, GROUPS, LANES), F32),
            jax.ShapeDtypeStruct((PROTOS, D), BF16),
        ),
        grid=(ROWS // BLOCK,),
        in_specs=[whole(a.shape) for a in rows + protos],
        out_specs=(
            pl.BlockSpec((BLOCK, PROTOS), lambda i: (i, 0)),
            whole((GROUPS, LANES)),
            whole((PEERS, GROUPS, LANES)),
            whole((PROTOS, D)),
        ),
        scratch_shapes=[pltpu.VMEM((ROWS, D), BF16)],
        compiler_params=params(),
        name="teacher_scores",
    )(*rows, *protos)


VMEM_SPEC = pl.BlockSpec(memory_space=pltpu.VMEM)
KERN_BLOCKS = ROWS // BLOCK


def weight_kernel(top_ref, got_ref, out_ref):
    got = got_ref[0]
    for peer in range(1, PEERS):
        got = jnp.maximum(got, got_ref[peer])
    out_ref[...] = jnp.exp(top_ref[...] - got)


def row_weight(top, got):
    return pl.pallas_call(
        weight_kernel,
        out_shape=jax.ShapeDtypeStruct((GROUPS, LANES), F32),
        in_specs=[VMEM_SPEC] * 2,
        out_specs=VMEM_SPEC,
        compiler_params=params(),
        name="row_weight",
    )(top, got)


def column_kernel(first, weight_ref, *refs):
    if first:
        kern_ref, sums_ref, acc_ref = refs
        scaled_ref = weight_ref
    else:
        got_ref, kern_ref, sums_ref, acc_ref, scaled_ref = refs
        scaled_ref[...] = weight_ref[...] / jnp.sum(got_ref[...], axis=0)
    acc_ref[...] = jnp.zeros_like(acc_ref)

    def step(block, carry):
        rows = pl.ds(pl.multiple_of(block * LANES, LANES), LANES)
        weight = down(scaled_ref[pl.ds(block, 1), :])
        for group in range(GROUPS):
            part = kern_ref[rows, group * LANES : (group + 1) * LANES].astype(F32) * weight
            acc_ref[group] += jnp.sum(part.reshape(LANES // 8, 8, LANES), axis=0)
        return carry

    lax.fori_loop(0, GROUPS, step, 0, unroll=UNROLL)
    for group in range(GROUPS):
        spread(sums_ref, 0, group, jnp.sum(acc_ref[group], axis=0, keepdims=True))


def column_pass(weight, kern, got=None):
    first = got is None
    scratch = [pltpu.VMEM((GROUPS, 8, LANES), F32)] + ([] if first else [pltpu.VMEM((GROUPS, LANES), F32)])
    inputs = (weight,) if first else (weight, got)
    return pl.pallas_call(
        functools.partial(column_kernel, first),
        out_shape=jax.ShapeDtypeStruct((Z * C, GROUPS, LANES), F32),
        in_specs=[VMEM_SPEC] * (len(inputs) + 1),
        out_specs=VMEM_SPEC,
        scratch_shapes=scratch,
        compiler_params=params(),
        name="column_pass",
    )(*inputs, in_vmem(kern))


def row_kernel(weight_ref, got_ref, kern_ref, sums_ref, scale_ref):
    scale_ref[...] = 1.0 / jnp.sum(got_ref[...], axis=0)

    def step(block, carry):
        rows = pl.ds(pl.multiple_of(block * LANES, LANES), LANES)
        weight = down(weight_ref[pl.ds(block, 1), :])
        total = jnp.zeros((LANES, LANES), F32)
        for group in range(GROUPS):
            part = kern_ref[rows, group * LANES : (group + 1) * LANES].astype(F32) * weight
            total += part * scale_ref[group : group + 1, :]
        spread(sums_ref, 0, block, along(total))
        return carry

    lax.fori_loop(0, GROUPS, step, 0, unroll=UNROLL)


def row_pass(weight, got, kern):
    return pl.pallas_call(
        row_kernel,
        out_shape=(
            jax.ShapeDtypeStruct((PEERS, GROUPS, LANES), F32),
            jax.ShapeDtypeStruct((GROUPS, LANES), F32),
        ),
        in_specs=[VMEM_SPEC] * 3,
        out_specs=(VMEM_SPEC, VMEM_SPEC),
        compiler_params=params(),
        name="row_pass",
    )(weight, got, in_vmem(kern))


def last_kernel(weight_ref, got_ref, protos_ref, *refs):
    rows_in, (kern_ref, sums_ref, scale_ref, rows_ref, scores_ref) = refs[:X], refs[X:]
    step = pl.program_id(0)

    @pl.when(step == 0)
    def _():
        place_rows(rows_in, rows_ref)
        scale_ref[...] = 1.0 / jnp.sum(got_ref[...], axis=0)

    rows = rows_ref[pl.ds(pl.multiple_of(step * BLOCK, BLOCK), BLOCK), :]
    scores_ref[...] = lax.dot_general(rows, protos_ref[...], TRANS_B, preferred_element_type=F32)
    for half in range(HALVES):
        weight = down(weight_ref[pl.ds(step * HALVES + half, 1), :])
        total = jnp.zeros((LANES, LANES), F32)
        crossed = jnp.zeros((LANES, LANES), F32)
        top = jnp.full((LANES, LANES), -jnp.inf, F32)
        for group in range(GROUPS):
            at = (slice(half * LANES, (half + 1) * LANES), slice(group * LANES, (group + 1) * LANES))
            part = (kern_ref[at].astype(F32) * weight) * scale_ref[group : group + 1, :]
            total += part
            scores = scores_ref[at]
            crossed += part * scores
            top = jnp.maximum(top, scores)
        top = jnp.max(jnp.transpose(top), axis=0, keepdims=True) * (S_SCALE * LOG2E)
        shift = down(top)
        spent = jnp.zeros((LANES, LANES), F32)
        for group in range(GROUPS):
            at = (slice(half * LANES, (half + 1) * LANES), slice(group * LANES, (group + 1) * LANES))
            spent += jnp.exp2(scores_ref[at] * (S_SCALE * LOG2E) - shift)
        spread(sums_ref, 0, step * HALVES + half, along(total))
        spread(sums_ref, GROUPS, step * HALVES + half, along(crossed) * S_SCALE)
        spread(sums_ref, 2 * GROUPS, step * HALVES + half, jnp.log2(along(spent)) + top)


def last_pass(weight, got, protos, rows, kern):
    return pl.pallas_call(
        last_kernel,
        out_shape=(
            jax.ShapeDtypeStruct((PEERS, 3 * GROUPS, LANES), F32),
            jax.ShapeDtypeStruct((GROUPS, LANES), F32),
            jax.ShapeDtypeStruct((ROWS, D), BF16),
        ),
        grid=(ROWS // BLOCK,),
        in_specs=[whole((GROUPS, LANES)), whole((Z * C, GROUPS, LANES)), whole((PROTOS, D))]
        + [whole(r.shape) for r in rows]
        + [pl.BlockSpec((BLOCK, PROTOS), lambda i: (i, 0))],
        out_specs=(
            whole((PEERS, 3 * GROUPS, LANES)),
            whole((GROUPS, LANES)),
            whole((ROWS, D)),
        ),
        scratch_shapes=[pltpu.VMEM((BLOCK, PROTOS), F32)],
        compiler_params=params(),
        name="last_pass",
    )(weight, got, protos, *rows, in_vmem(kern))


def grad_kernel(
    weight_ref, got_ref, scale_ref, kern_ref, rows_ref, protos_ref,
    student_ref, keep_ref, send_ref, loss_ref, scaled_ref, lse_ref, scores_ref, logits_ref, acc_ref,
):
    step = pl.program_id(0)

    @pl.when(step == 0)
    def _():
        sums = jnp.sum(got_ref[:, :GROUPS, :], axis=0)
        crossed = jnp.sum(got_ref[:, GROUPS : 2 * GROUPS, :], axis=0)
        top = got_ref[0, 2 * GROUPS :, :]
        for peer in range(1, PEERS):
            top = jnp.maximum(top, got_ref[peer, 2 * GROUPS :, :])
        total = jnp.zeros_like(top)
        for peer in range(PEERS):
            total += jnp.exp2(got_ref[peer, 2 * GROUPS :, :] - top)
        lse = top + jnp.log2(total)
        lse_ref[...] = lse - math.log2(GRAD_SCALE)
        scaled_ref[...] = weight_ref[...] / sums * GRAD_SCALE
        terms = (lse * math.log(2.0) * sums - crossed) / sums
        terms = jnp.sum(jnp.sum(terms, axis=0, keepdims=True), axis=1, keepdims=True)
        loss_ref[...] = jnp.broadcast_to(terms, (8, LANES))
        acc_ref[...] = jnp.zeros_like(acc_ref)

    rows = rows_ref[...]
    scores_ref[...] = lax.dot_general(rows, protos_ref[...], TRANS_B, preferred_element_type=F32)
    for half in range(HALVES):
        weight = down(scaled_ref[pl.ds(step * HALVES + half, 1), :])
        lse = down(lse_ref[pl.ds(step * HALVES + half, 1), :])
        for group in range(GROUPS):
            at = (slice(half * LANES, (half + 1) * LANES), slice(group * LANES, (group + 1) * LANES))
            target = (kern_ref[at].astype(F32) * weight) * scale_ref[group : group + 1, :]
            prob = jnp.exp2(scores_ref[at] * (S_SCALE * LOG2E) - lse)
            logits_ref[at] = (prob - target).astype(BF16)
    logits = logits_ref[...]
    student_ref[...] = jnp.dot(logits, protos_ref[...], preferred_element_type=F32).astype(BF16)
    acc_ref[...] += jnp.dot(jnp.transpose(rows), logits, preferred_element_type=F32)

    @pl.when(step == pl.num_programs(0) - 1)
    def _():
        core = lax.axis_index("c")
        for z in range(Z):
            for c in range(C):
                first = (z * C + c) * OWN_PROTOS
                part = jnp.transpose(acc_ref[:, first : first + OWN_PROTOS])

                @pl.when(core == c)
                def _(part=part, z=z):
                    keep_ref[z] = part

                @pl.when(core != c)
                def _(part=part, z=z):
                    send_ref[z] = part.astype(BF16)


def gradients(weight, got, scale, kern, rows, protos):
    return pl.pallas_call(
        grad_kernel,
        out_shape=(
            pltpu.HBM((ROWS, D), BF16),
            jax.ShapeDtypeStruct((Z, OWN_PROTOS, D), F32),
            jax.ShapeDtypeStruct((Z, OWN_PROTOS, D), BF16),
            jax.ShapeDtypeStruct((8, LANES), F32),
        ),
        grid=(ROWS // BLOCK,),
        in_specs=[
            whole(weight.shape),
            whole(got.shape),
            whole(scale.shape),
            pl.BlockSpec((BLOCK, PROTOS), lambda i: (i, 0)),
            pl.BlockSpec((BLOCK, D), lambda i: (i, 0)),
            whole((PROTOS, D)),
        ],
        out_specs=(
            pl.BlockSpec((BLOCK, D), lambda i: (i, 0)),
            whole((Z, OWN_PROTOS, D)),
            whole((Z, OWN_PROTOS, D)),
            whole((8, LANES)),
        ),
        scratch_shapes=[
            pltpu.VMEM((GROUPS, LANES), F32),
            pltpu.VMEM((GROUPS, LANES), F32),
            pltpu.VMEM((BLOCK, PROTOS), F32),
            pltpu.VMEM((BLOCK, PROTOS), BF16),
            pltpu.VMEM((D, PROTOS), F32),
        ],
        compiler_params=params(),
        name="gradients",
    )(weight, got, scale, in_vmem(kern), rows, protos)


TAIL = 16


def split_kernel(keep_ref, got_ref, loss_ref, other_ref, mine_ref, *outs):
    value = jnp.broadcast_to((loss_ref[...] + other_ref[...])[0:1, :], (TAIL, LANES))
    high = value.astype(BF16)
    rest = value - high.astype(F32)
    middle = rest.astype(BF16)
    low = (rest - middle.astype(F32)).astype(BF16)
    row = lax.broadcasted_iota(jnp.int32, (TAIL, LANES), 0)
    tail = jnp.where(row == 0, high.astype(F32), jnp.where(row == 1, middle.astype(F32), low.astype(F32)))
    tail = jnp.concatenate([tail, tail], axis=1).astype(BF16)
    for shift, out in enumerate(outs):
        at = lax.rem(lax.axis_index("z") + shift, Z)
        part = keep_ref[at] + got_ref[at].astype(F32)
        if shift == 0:
            mine_ref[...] = part
        out[:OWN_PROTOS, :] = part.astype(BF16)
        out[OWN_PROTOS:, :] = tail


def split_sums(keep, got, loss, other):
    return pl.pallas_call(
        split_kernel,
        out_shape=(jax.ShapeDtypeStruct((OWN_PROTOS, D), F32),)
        + (jax.ShapeDtypeStruct((OWN_PROTOS + TAIL, D), BF16),) * Z,
        in_specs=[VMEM_SPEC] * 4,
        out_specs=(VMEM_SPEC,) * (Z + 1),
        compiler_params=params(),
        name="split_sums",
    )(keep, got, loss, other)


def join_kernel(mine_ref, *refs):
    parts, (out_ref, loss_ref, value_ref) = refs[:Z], refs[Z:]
    total = mine_ref[...]
    for shift, part in enumerate(parts):
        if shift:
            total += part[:OWN_PROTOS, :].astype(F32)
        tail = part[OWN_PROTOS:, :LANES].astype(F32)
        at = lax.rem(lax.axis_index("z") + Z - shift, Z)
        value_ref[pl.ds(at, 1), :] = tail[0:1] + (tail[1:2] + tail[2:3])
    out_ref[...] = total
    loss = value_ref[0:1, :]
    for z in range(1, Z):
        loss = loss + value_ref[z : z + 1, :]
    loss_ref[...] = jnp.broadcast_to(loss, (8, LANES)) * (1.0 / TOTAL_ROWS)


def join_sums(mine, parts):
    return pl.pallas_call(
        join_kernel,
        out_shape=(jax.ShapeDtypeStruct((OWN_PROTOS, D), F32), jax.ShapeDtypeStruct((8, LANES), F32)),
        in_specs=[VMEM_SPEC] * (Z + 1),
        out_specs=(VMEM_SPEC, VMEM_SPEC),
        scratch_shapes=[pltpu.VMEM((Z, LANES), F32)],
        compiler_params=params(),
        name="join_sums",
    )(mine, *parts)


def shift_x(value, by):
    return lax.ppermute(value, "x", [(i, (i + by) % X) for i in range(X)])


def shift_z(value, by):
    return lax.ppermute(value, "z", [(i, (i + by) % Z) for i in range(Z)])


def swap_core(value):
    return lax.ppermute(value, "c", [(0, 1), (1, 0)])


def fan_z(value, by):
    pairs = [(z * C + c, (z + (by if c == 0 else -by)) % Z * C + c) for z in range(Z) for c in range(C)]
    return lax.ppermute(value, ("z", "c"), pairs)


def over_rows(parts):
    return lax.all_to_all(parts, ("x", "y"), 0, 0, tiled=True)


def over_protos(parts):
    return lax.all_to_all(parts, ("z", "c"), 0, 0, tiled=True)


def over_y(parts):
    return lax.all_to_all(parts, "y", 0, 0, tiled=True)


def body(teacher_tokens, student_tokens, masked_index, prototypes):
    teacher_rows = pick_rows(masked_index, teacher_tokens)
    student_rows = pick_rows(masked_index, student_tokens)
    teacher_rows, student_rows, prototypes = lax.optimization_barrier((teacher_rows, student_rows, prototypes))
    other = swap_core(prototypes)
    far_own = shift_z(prototypes, Z // 2)
    teacher_in = [teacher_rows] + [shift_x(teacher_rows, by) for by in (2, 1, -1)]
    chip_protos = jnp.concatenate([prototypes, other], axis=0)
    near = [fan_z(chip_protos, by) for by in (1, 2, 3)]
    protos_in = [chip_protos, *near, *[swap_core(part) for part in near], far_own, swap_core(far_own)]
    student_in = [student_rows] + [shift_x(student_rows, by) for by in (2, 1, -1)]
    kern, top, tops, protos = teacher_scores(teacher_in, protos_in)
    weight = row_weight(top, over_rows(tops))
    weight, student_in = lax.optimization_barrier((weight, student_in))
    sums = column_pass(weight, kern)
    got, _ = row_pass(weight, over_protos(sums), kern)
    sums = column_pass(weight, kern, over_rows(got))
    got, _ = row_pass(weight, over_protos(sums), kern)
    sums = column_pass(weight, kern, over_rows(got))
    got, scale, rows = last_pass(weight, over_protos(sums), protos, student_in, kern)
    student, keep, send, loss = gradients(weight, over_rows(got), scale, kern, rows, protos)

    mine, own, *sends = split_sums(keep, swap_core(send), loss, swap_core(loss))
    parts = [own] + [None] * (Z - 1)
    for by in (4, 3, 5, 2, 6, 1, 7):
        parts[by] = shift_z(sends[by - 1], by)
    student = over_rows(student.reshape(PEERS, ROWS // PEERS, D))
    student, parts[1:] = lax.optimization_barrier((student, parts[1:]))
    student = jnp.sum(student.astype(F32), axis=0).astype(BF16)
    student = over_y(jnp.broadcast_to(student[None], (Y,) + student.shape))
    grad_weight, loss = join_sums(mine, parts)
    return loss[0, 0], student.reshape(OWN_ROWS, D), grad_weight


def solution(mesh):
    named = Mesh(mesh.devices.reshape(X, Z, C, Y), ("x", "z", "c", "y"))
    batch = ("x", "z", "c")
    placed = (
        P(batch, None, None),
        P(batch, None, None),
        P(batch, None),
        P((*batch, "y"), None),
    )
    return jax.shard_map(
        body,
        mesh=named,
        in_specs=placed,
        out_specs=(P(), P(batch, None), P((*batch, "y"), None)),
        check_vma=False,
    )
```

time: 1130 us -> 207 us (0.18)
  blocking collectives: 876 us -> 85.5 us
  waiting for transfers between devices: 117 us -> 21 us
  other arithmetic: 80 us -> 0.14 us
  starting transfers between devices: 0.08 us -> 49.7 us
  Pallas kernels: 0 us -> 41.8 us
  matrix products: 28.1 us -> 0 us
  between operations: 16.5 us -> 0.78 us
    psum x8 -> x0, blocking collectives: 858 us -> none  [the longest x3 739 us: column_scale(): return 1.0 / lax.psum(partial_value, 'batch')]
    all_to_all x0 -> x7, blocking collectives: none -> 85.5 us  [the longest x4 50.5 us: over_rows(): return lax.all_to_all(parts, ('x', 'y'), 0, 0, tiled=True)]
    all_gather x1 -> x0, waiting for transfers between devices: 72.9 us -> none  [body(): gathered = lax.all_gather(prototypes, 'batch', axis=0, tiled=True)]
    reduce_sum x6 -> x1, other arithmetic: 56.1 us -> 0.14 us  [body(): student = jnp.sum(student.astype(F32), axis=0).astype(BF16)]
    reduce_scatter x1 -> x0, waiting for transfers between devices: 43.3 us -> none  [body(): lax.psum_scatter(lax.dot_general(grad_logits, student_rows, (((0,), (0,))...]
    pallas_call x0 -> x13, Pallas kernels: none -> 41.8 us  [the longest x1 13.8 us: gradients(): pl.pallas_call(grad_kernel, out_shape=(pltpu.HBM((ROWS, D), BF16), jax.Sh...]
    ppermute x0 -> x24, starting transfers between devices: none -> 40 us  [the longest x8 21.3 us: shift_z(): return lax.ppermute(value, 'z', [(i, (i + by) % Z) for i in range(Z)])]
    dot_general x3 -> x0, matrix products: 28.1 us -> none  [the longest x1 15.6 us: body(): lax.dot_general(stacked, gathered, contract, preferred_element_type=jnp.f...]
  transfers between devices with their start and end apart: 2 -> 26, of which waited for: 2 -> 11; matrix products, arithmetic and copies ran while one was open for 2% -> 1% of each run, Pallas kernels for 0% -> 4%
where the time goes in v2:
time: 207 us; the launch traced here: 205 us
  blocking collectives  85.5 us (41%)
  starting transfers between devices  49.7 us (24%)
  Pallas kernels  41.8 us (20%)
  waiting for transfers between devices  21 us (10%)
  local copies, waits for them, and re-layouts  5.94 us (3%)
    all_to_all x4, blocking collectives, over_rows(): return lax.all_to_all(parts, ('x', 'y'), 0, 0, tiled=True)  50.5 us
    all_to_all x3, blocking collectives, over_protos(): return lax.all_to_all(parts, ('z', 'c'), 0, 0, tiled=True)  35 us
    ppermute x8, starting transfers between devices, shift_z(): return lax.ppermute(value, 'z', [(i, (i + by) % Z) for i in range(Z)])  21.3 us
    pallas_call x1, Pallas kernels, gradients(): pl.pallas_call(grad_kernel, out_shape=(pltpu.HBM((ROWS, D), BF16), jax.Sh...  13.8 us
    pallas_call x1, Pallas kernels, last_pass(): pl.pallas_call(last_kernel, out_shape=(jax.ShapeDtypeStruct((PEERS, 3 * G...  9.81 us
    ppermute x6, starting transfers between devices, shift_x(): return lax.ppermute(value, 'x', [(i, (i + by) % X) for i in range(X)])  9.01 us
    ppermute x8, waiting for transfers between devices, shift_z(): return lax.ppermute(value, 'z', [(i, (i + by) % Z) for i in range(Z)])  8.89 us
    ppermute x3, starting transfers between devices, fan_z(): return lax.ppermute(value, ('z', 'c'), pairs)  8.46 us
  transfers between devices with their start and end apart: 26, of which 11 were waited for; matrix products, arithmetic and copies ran while one was open for 1% of the time, Pallas kernels for 4%

profile of v2, /device:TPU:8, one launch (start us, length us, event | category | flops | bytes accessed | tf_op | source)
XLA Modules:
  0.0 204.9 jit_solution(8657808269727441585)
XLA Ops:
  4.5 7.3 %collective-permute-start.10 = (bf16[128,256]{1,0:T(8,128)(2,1)}, bf16[128,256]{1,0:T(8,128)(2,1)S(1)}, u32[]{:S(2)}, u32[]{:S(2)}) collective-permute-start(bf16[128,256]{1,0:T(8,128)(2,1)} %param.7), channel_id=1, source_target_pairs={{0,32},{8,40},{16,48},{24,56},{32,0},{40,8},{48,16},{56,24},{1,33}... | collective-permute-start | bytes 196616 | tf_op jit(solution)/shard_map/ppermute | solution.py:450
  12.6 1.9 collective-permute-done.10.refs_11_
  14.5 3.1 %collective-permute-start.6 = (bf16[256,256]{1,0:T(8,128)(2,1)S(1)}, bf16[256,256]{1,0:T(8,128)(2,1)S(1)}, u32[]{:S(2)}, u32[]{:S(2)}) collective-permute-start(bf16[256,256]{1,0:T(8,128)(2,1)S(1)} %constant_dynamic-update-slice_fusion.refs_4_), channel_id=1, source_target_pairs={{0,24},{4,44},{8,32},{12,52},{16,40},{20,60},{24,48},{28,4},{32,56... | collective-permute-start | bytes 393224 | tf_op jit(solution)/shard_map/ppermute | solution.py:459
  17.7 2.8 %collective-permute-start.2 = (bf16[512,256]{1,0:T(8,128)(2,1)S(1)}, bf16[512,256]{1,0:T(8,128)(2,1)S(1)}, u32[]{:S(2)}, u32[]{:S(2)}) collective-permute-start(bf16[512,256]{1,0:T(8,128)(2,1)S(1)} %pick_rows.2.refs_0_), channel_id=1, source_target_pairs={{0,192},{64,0},{128,64},{192,128},{1,193},{65,1},{129,65},{193,129... | collective-permute-start | bytes 786440 | tf_op jit(solution)/shard_map/ppermute | solution.py:446
  20.4 2.3 %collective-permute-start = (bf16[512,256]{1,0:T(8,128)(2,1)S(1)}, bf16[512,256]{1,0:T(8,128)(2,1)S(1)}, u32[]{:S(2)}, u32[]{:S(2)}) collective-permute-start(bf16[512,256]{1,0:T(8,128)(2,1)S(1)} %pick_rows.2.refs_0_), channel_id=1, source_target_pairs={{0,128},{64,192},{128,0},{192,64},{1,129},{65,193},{129,1},{193,65... | collective-permute-start | bytes 786440 | tf_op jit(solution)/shard_map/ppermute | solution.py:446
  22.7 5.0 %collective-permute-start.5 = (bf16[256,256]{1,0:T(8,128)(2,1)S(1)}, bf16[256,256]{1,0:T(8,128)(2,1)S(1)}, u32[]{:S(2)}, u32[]{:S(2)}) collective-permute-start(bf16[256,256]{1,0:T(8,128)(2,1)S(1)} %constant_dynamic-update-slice_fusion.refs_4_), channel_id=1, source_target_pairs={{0,16},{4,52},{8,24},{12,60},{16,32},{20,4},{24,40},{28,12},{32,48... | collective-permute-start | bytes 393224 | tf_op jit(solution)/shard_map/ppermute | solution.py:459
  28.0 3.6 %collective-permute-done.5.refs_6_ = bf16[256,256]{1,0:T(8,128)(2,1)S(1)} collective-permute-done((bf16[256,256]{1,0:T(8,128)(2,1)S(1)}, bf16[256,256]{1,0:T(8,128)(2,1)S(1)}, u32[]{:S(2)}, u32[]{:S(2)}) %collective-permute-start.5) | collective-permute-done | bytes 131104 | tf_op jit(solution)/shard_map/ppermute | solution.py:459
  31.8 2.1 %collective-permute-done.4.refs_5_ = bf16[256,256]{1,0:T(8,128)(2,1)S(1)} collective-permute-done((bf16[256,256]{1,0:T(8,128)(2,1)S(1)}, bf16[256,256]{1,0:T(8,128)(2,1)S(1)}, u32[]{:S(2)}, u32[]{:S(2)}) %collective-permute-start.4) | collective-permute-done | bytes 131104 | tf_op jit(solution)/shard_map/ppermute | solution.py:459
  35.9 1.9 collective-permute-start.12
  39.4 6.4 %teacher_scores.1 = (bf16[2048,2048]{1,0:T(8,128)(2,1)S(1)}, f32[16,128]{1,0:T(8,128)S(1)}, f32[16,16,128]{2,1,0:T(8,128)S(1)}, bf16[2048,256]{1,0:T(8,128)(2,1)S(1)}) custom-call(bf16[512,256]{1,0:T(8,128)(2,1)S(1)} %pick_rows.2.refs_0_, bf16[512,256]{1,0:T(8,128)(2,1)S(1)} %collective-permute-done.refs_1_, ...), custom_call_target="tpu_custom_call" | custom-call | tf_op jit(solution)/shard_map/teacher_scores/pallas_call | solution.py:125
  45.8 13.1 %all_to_all.45.got_ref = f32[16,16,128]{2,1,0:T(8,128)S(1)} all-to-all(f32[16,16,128]{2,1,0:T(8,128)S(1)} %get-tuple-element.46), channel_id=1, replica_groups=mesh['x'=4,'z'=8,'c'=2,'y'=4] {'x','y'}, dimensions={0} | all-to-all | bytes 262144 | tf_op jit(solution)/shard_map/all_to_all | solution.py:463
  60.7 12.4 %all_to_all.46.got_ref = f32[16,16,128]{2,1,0:T(8,128)S(1)} all-to-all(f32[16,16,128]{2,1,0:T(8,128)S(1)} %column_pass.3), channel_id=1, replica_groups=mesh['x'=4,'z'=8,'c'=2,'y'=4] {'z','c'}, dimensions={0} | all-to-all | bytes 262144 | tf_op jit(solution)/shard_map/all_to_all | solution.py:467
  73.0 2.4 %row_pass.2 = (f32[16,16,128]{2,1,0:T(8,128)S(1)}, f32[16,128]{1,0:T(8,128)}) custom-call(f32[16,128]{1,0:T(8,128)S(1)} %row_weight.1.weight_ref, f32[16,16,128]{2,1,0:T(8,128)S(1)} %all_to_all.46.got_ref, bf16[2048,2048]{1,0:T(8,128)(2,1)S(1)} %get-tuple-element.49.refs_0_.kern_ref.refs_1_.refs_4_), custom_call_target="tpu_custom_call" | custom-call | tf_op jit(solution)/shard_map/row_pass/pallas_call | solution.py:223
  75.5 11.6 %all_to_all.47.refs_0_ = f32[16,16,128]{2,1,0:T(8,128)S(1)} all-to-all(f32[16,16,128]{2,1,0:T(8,128)S(1)} %get-tuple-element.50), channel_id=1, replica_groups=mesh['x'=4,'z'=8,'c'=2,'y'=4] {'x','y'}, dimensions={0} | all-to-all | bytes 262144 | tf_op jit(solution)/shard_map/all_to_all | solution.py:463
  87.1 1.8 column_pass.4
  88.9 11.3 %all_to_all.48.got_ref = f32[16,16,128]{2,1,0:T(8,128)S(1)} all-to-all(f32[16,16,128]{2,1,0:T(8,128)S(1)} %column_pass.4), channel_id=1, replica_groups=mesh['x'=4,'z'=8,'c'=2,'y'=4] {'z','c'}, dimensions={0} | all-to-all | bytes 262144 | tf_op jit(solution)/shard_map/all_to_all | solution.py:467
  100.2 2.4 %row_pass.3 = (f32[16,16,128]{2,1,0:T(8,128)S(1)}, f32[16,128]{1,0:T(8,128)}) custom-call(f32[16,128]{1,0:T(8,128)S(1)} %row_weight.1.weight_ref, f32[16,16,128]{2,1,0:T(8,128)S(1)} %all_to_all.48.got_ref, bf16[2048,2048]{1,0:T(8,128)(2,1)S(1)} %get-tuple-element.49.refs_0_.kern_ref.refs_1_.refs_4_), custom_call_target="tpu_custom_call" | custom-call | tf_op jit(solution)/shard_map/row_pass/pallas_call | solution.py:223
  102.6 11.5 %all_to_all.49.refs_0_ = f32[16,16,128]{2,1,0:T(8,128)S(1)} all-to-all(f32[16,16,128]{2,1,0:T(8,128)S(1)} %get-tuple-element.51), channel_id=1, replica_groups=mesh['x'=4,'z'=8,'c'=2,'y'=4] {'x','y'}, dimensions={0} | all-to-all | bytes 262144 | tf_op jit(solution)/shard_map/all_to_all | solution.py:463
  116.0 11.3 %all_to_all.50.got_ref = f32[16,16,128]{2,1,0:T(8,128)S(1)} all-to-all(f32[16,16,128]{2,1,0:T(8,128)S(1)} %column_pass.5), channel_id=1, replica_groups=mesh['x'=4,'z'=8,'c'=2,'y'=4] {'z','c'}, dimensions={0} | all-to-all | bytes 262144 | tf_op jit(solution)/shard_map/all_to_all | solution.py:467
  127.3 9.8 %last_pass.1 = (f32[16,48,128]{2,1,0:T(8,128)S(1)}, f32[16,128]{1,0:T(8,128)S(1)}, bf16[2048,256]{1,0:T(8,128)(2,1)S(1)}) custom-call(f32[16,128]{1,0:T(8,128)S(1)} %row_weight.1.weight_ref, f32[16,16,128]{2,1,0:T(8,128)S(1)} %all_to_all.50.got_ref, bf16[2048,256]{1,0:T(8,128)(2,1)S(1)} %get-tuple-element.52.protos_ref, ...), custom_call_target="tpu_custom_call" | custom-call | tf_op jit(solution)/shard_map/last_pass/pallas_call | solution.py:271
  137.1 14.3 %all_to_all.51.got_ref = f32[16,48,128]{2,1,0:T(8,128)S(1)} all-to-all(f32[16,48,128]{2,1,0:T(8,128)S(1)} %get-tuple-element.57), channel_id=1, replica_groups=mesh['x'=4,'z'=8,'c'=2,'y'=4] {'x','y'}, dimensions={0} | all-to-all | bytes 786432 | tf_op jit(solution)/shard_map/all_to_all | solution.py:463
  151.4 13.8 %gradients.1 = (bf16[2048,256]{1,0:T(8,128)(2,1)}, f32[8,128,256]{2,1,0:T(8,128)S(1)}, bf16[8,128,256]{2,1,0:T(8,128)(2,1)S(1)}, f32[8,128]{1,0:T(8,128)S(1)}) custom-call(f32[16,128]{1,0:T(8,128)S(1)} %row_weight.1.weight_ref, f32[16,48,128]{2,1,0:T(8,128)S(1)} %all_to_all.51.got_ref, f32[16,128]{1,0:T(8,128)S(1)} %get-tuple-element.58.scale_ref, ...), custom_call_target="tpu_custom_call" | custom-call | tf_op jit(solution)/shard_map/gradients/pallas_call | solution.py:349
  165.3 4.9 %all-to-all-start.7 = ((bf16[16,128,256]{2,1,0:T(8,128)(2,1)}), bf16[16,128,256]{2,1,0:T(8,128)(2,1)S(1)}, u32[]{:S(2)}, u32[]{:S(2)}) async-start(bf16[16,128,256]{2,1,0:T(8,128)(2,1)} %bitcast.3), calls=%async_computation.7 | async-start | bytes 2097152 | tf_op jit(solution)/shard_map/all_to_all | solution.py:463
  173.6 2.2 %collective-permute-start.19 = (bf16[144,256]{1,0:T(8,128)(2,1)S(1)}, bf16[144,256]{1,0:T(8,128)(2,1)S(1)}, u32[]{:S(2)}, u32[]{:S(2)}) collective-permute-start(bf16[144,256]{1,0:T(8,128)(2,1)S(1)} %get-tuple-element.68), channel_id=1, source_target_pairs={{0,24},{8,32},{16,40},{24,48},{32,56},{40,0},{48,8},{56,16},{1,25}... | collective-permute-start | bytes 221192 | tf_op jit(solution)/shard_map/ppermute | solution.py:450
  175.8 3.5 %collective-permute-start.20 = (bf16[144,256]{1,0:T(8,128)(2,1)S(1)}, bf16[144,256]{1,0:T(8,128)(2,1)S(1)}, u32[]{:S(2)}, u32[]{:S(2)}) collective-permute-start(bf16[144,256]{1,0:T(8,128)(2,1)S(1)} %get-tuple-element.69), channel_id=1, source_target_pairs={{0,32},{8,40},{16,48},{24,56},{32,0},{40,8},{48,16},{56,24},{1,33}... | collective-permute-start | bytes 221192 | tf_op jit(solution)/shard_map/ppermute | solution.py:450
  179.3 1.9 collective-permute-start.21
  181.2 2.1 %collective-permute-start.22 = (bf16[144,256]{1,0:T(8,128)(2,1)S(1)}, bf16[144,256]{1,0:T(8,128)(2,1)S(1)}, u32[]{:S(2)}, u32[]{:S(2)}) collective-permute-start(bf16[144,256]{1,0:T(8,128)(2,1)S(1)} %get-tuple-element.71), channel_id=1, source_target_pairs={{0,48},{8,56},{16,0},{24,8},{32,16},{40,24},{48,32},{56,40},{1,49}... | collective-permute-start | bytes 221192 | tf_op jit(solution)/shard_map/ppermute | solution.py:450
  183.3 2.9 %collective-permute-start.23 = (bf16[144,256]{1,0:T(8,128)(2,1)S(1)}, bf16[144,256]{1,0:T(8,128)(2,1)S(1)}, u32[]{:S(2)}, u32[]{:S(2)}) collective-permute-start(bf16[144,256]{1,0:T(8,128)(2,1)S(1)} %get-tuple-element.72), channel_id=1, source_target_pairs={{0,56},{8,0},{16,8},{24,16},{32,24},{40,32},{48,40},{56,48},{1,57}... | collective-permute-start | bytes 221192 | tf_op jit(solution)/shard_map/ppermute | solution.py:450
  186.5 2.1 %collective-permute-done.21.refs_5_ = bf16[144,256]{1,0:T(8,128)(2,1)S(1)} collective-permute-done((bf16[144,256]{1,0:T(8,128)(2,1)S(1)}, bf16[144,256]{1,0:T(8,128)(2,1)S(1)}, u32[]{:S(2)}, u32[]{:S(2)}) %collective-permute-start.21) | collective-permute-done | bytes 73760 | tf_op jit(solution)/shard_map/ppermute | solution.py:450
  188.6 4.3 %collective-permute-done.22.refs_6_ = bf16[144,256]{1,0:T(8,128)(2,1)S(1)} collective-permute-done((bf16[144,256]{1,0:T(8,128)(2,1)S(1)}, bf16[144,256]{1,0:T(8,128)(2,1)S(1)}, u32[]{:S(2)}, u32[]{:S(2)}) %collective-permute-start.22) | collective-permute-done | bytes 73760 | tf_op jit(solution)/shard_map/ppermute | solution.py:450
  194.1 4.8 %all-to-all-start.8 = ((bf16[4,128,256]{2,1,0:T(8,128)(2,1)}), bf16[4,128,256]{2,1,0:T(8,128)(2,1)S(1)}, u32[]{:S(2)}, u32[]{:S(2)}) async-start(bf16[4,128,256]{2,1,0:T(8,128)(2,1)} %broadcast_in_dim.2), calls=%async_computation.8 | async-start | bytes 524288 | tf_op jit(solution)/shard_map/all_to_all | solution.py:471
  200.2 4.0 %all-to-all-done.8 = bf16[4,128,256]{2,1,0:T(8,128)(2,1)S(1)} async-done(((bf16[4,128,256]{2,1,0:T(8,128)(2,1)}), bf16[4,128,256]{2,1,0:T(8,128)(2,1)S(1)}, u32[]{:S(2)}, u32[]{:S(2)}) %all-to-all-start.8) | async-done | bytes 262176 | tf_op jit(solution)/shard_map/all_to_all | solution.py:471
  (52 shorter events, 19.2 us)
Async XLA Ops:
  0.6 1.2 copy-start
  1.9 0.7 copy-start.2
  2.9 1.2 copy-start.1
  4.5 10.0 %collective-permute-start.10 = (bf16[128,256]{1,0:T(8,128)(2,1)}, bf16[128,256]{1,0:T(8,128)(2,1)S(1)}, u32[]{:S(2)}, u32[]{:S(2)}) collective-permute-start(bf16[128,256]{1,0:T(8,128)(2,1)} %param.7), channel_id=1, source_target_pairs={{0,32},{8,40},{16,48},{24,56},{32,0},{40,8},{48,16},{56,24},{1,33}... | collective-permute-start | bytes 196616 | tf_op jit(solution)/shard_map/ppermute | solution.py:450
  11.7 2.8 %collective-permute-start.3 = (bf16[128,256]{1,0:T(8,128)(2,1)}, bf16[128,256]{1,0:T(8,128)(2,1)S(1)}, u32[]{:S(2)}, u32[]{:S(2)}) collective-permute-start(bf16[128,256]{1,0:T(8,128)(2,1)} %param.7), channel_id=1, source_target_pairs={{0,4},{4,0},{1,5},{5,1},{2,6},{6,2},{3,7},{7,3},{8,12},{12,8},{9,1... | collective-permute-start | bytes 196616 | tf_op jit(solution)/shard_map/ppermute | solution.py:454
  14.5 8.2 %collective-permute-start.11 = (bf16[128,256]{1,0:T(8,128)(2,1)S(1)}, bf16[128,256]{1,0:T(8,128)(2,1)S(1)}, u32[]{:S(2)}, u32[]{:S(2)}) collective-permute-start(bf16[128,256]{1,0:T(8,128)(2,1)S(1)} %collective-permute-done.10.refs_11_), channel_id=1, source_target_pairs={{0,4},{4,0},{1,5},{5,1},{2,6},{6,2},{3,7},{7,3},{8,12},{12,8},{9,1... | collective-permute-start | bytes 196616 | tf_op jit(solution)/shard_map/ppermute | solution.py:454
  14.5 13.2 %collective-permute-start.6 = (bf16[256,256]{1,0:T(8,128)(2,1)S(1)}, bf16[256,256]{1,0:T(8,128)(2,1)S(1)}, u32[]{:S(2)}, u32[]{:S(2)}) collective-permute-start(bf16[256,256]{1,0:T(8,128)(2,1)S(1)} %constant_dynamic-update-slice_fusion.refs_4_), channel_id=1, source_target_pairs={{0,24},{4,44},{8,32},{12,52},{16,40},{20,60},{24,48},{28,4},{32,56... | collective-permute-start | bytes 393224 | tf_op jit(solution)/shard_map/ppermute | solution.py:459
  17.7 17.4 %collective-permute-start.2 = (bf16[512,256]{1,0:T(8,128)(2,1)S(1)}, bf16[512,256]{1,0:T(8,128)(2,1)S(1)}, u32[]{:S(2)}, u32[]{:S(2)}) collective-permute-start(bf16[512,256]{1,0:T(8,128)(2,1)S(1)} %pick_rows.2.refs_0_), channel_id=1, source_target_pairs={{0,192},{64,0},{128,64},{192,128},{1,193},{65,1},{129,65},{193,129... | collective-permute-start | bytes 786440 | tf_op jit(solution)/shard_map/ppermute | solution.py:446
  20.4 15.5 %collective-permute-start.1 = (bf16[512,256]{1,0:T(8,128)(2,1)S(1)}, bf16[512,256]{1,0:T(8,128)(2,1)S(1)}, u32[]{:S(2)}, u32[]{:S(2)}) collective-permute-start(bf16[512,256]{1,0:T(8,128)(2,1)S(1)} %pick_rows.2.refs_0_), channel_id=1, source_target_pairs={{0,64},{64,128},{128,192},{192,0},{1,65},{65,129},{129,193},{193,1... | collective-permute-start | bytes 786440 | tf_op jit(solution)/shard_map/ppermute | solution.py:446
  20.4 17.4 %collective-permute-start = (bf16[512,256]{1,0:T(8,128)(2,1)S(1)}, bf16[512,256]{1,0:T(8,128)(2,1)S(1)}, u32[]{:S(2)}, u32[]{:S(2)}) collective-permute-start(bf16[512,256]{1,0:T(8,128)(2,1)S(1)} %pick_rows.2.refs_0_), channel_id=1, source_target_pairs={{0,128},{64,192},{128,0},{192,64},{1,129},{65,193},{129,1},{193,65... | collective-permute-start | bytes 786440 | tf_op jit(solution)/shard_map/ppermute | solution.py:446
  22.7 8.9 %collective-permute-start.5 = (bf16[256,256]{1,0:T(8,128)(2,1)S(1)}, bf16[256,256]{1,0:T(8,128)(2,1)S(1)}, u32[]{:S(2)}, u32[]{:S(2)}) collective-permute-start(bf16[256,256]{1,0:T(8,128)(2,1)S(1)} %constant_dynamic-update-slice_fusion.refs_4_), channel_id=1, source_target_pairs={{0,16},{4,52},{8,24},{12,60},{16,32},{20,4},{24,40},{28,12},{32,48... | collective-permute-start | bytes 393224 | tf_op jit(solution)/shard_map/ppermute | solution.py:459
  27.7 6.2 %collective-permute-start.4 = (bf16[256,256]{1,0:T(8,128)(2,1)S(1)}, bf16[256,256]{1,0:T(8,128)(2,1)S(1)}, u32[]{:S(2)}, u32[]{:S(2)}) collective-permute-start(bf16[256,256]{1,0:T(8,128)(2,1)S(1)} %constant_dynamic-update-slice_fusion.refs_4_), channel_id=1, source_target_pairs={{0,8},{4,60},{8,16},{12,4},{16,24},{20,12},{24,32},{28,20},{32,40}... | collective-permute-start | bytes 393224 | tf_op jit(solution)/shard_map/ppermute | solution.py:459
  31.6 6.2 %collective-permute-start.9 = (bf16[256,256]{1,0:T(8,128)(2,1)S(1)}, bf16[256,256]{1,0:T(8,128)(2,1)S(1)}, u32[]{:S(2)}, u32[]{:S(2)}) collective-permute-start(bf16[256,256]{1,0:T(8,128)(2,1)S(1)} %collective-permute-done.6.refs_7_), channel_id=1, source_target_pairs={{0,4},{4,0},{1,5},{5,1},{2,6},{6,2},{3,7},{7,3},{8,12},{12,8},{9,1... | collective-permute-start | bytes 393224 | tf_op jit(solution)/shard_map/ppermute | solution.py:454
  33.9 25.0 %collective-permute-start.14 = (bf16[512,256]{1,0:T(8,128)(2,1)S(1)}, bf16[512,256]{1,0:T(8,128)(2,1)S(1)}, u32[]{:S(2)}, u32[]{:S(2)}) collective-permute-start(bf16[512,256]{1,0:T(8,128)(2,1)S(1)} %pick_rows.3.refs_0_), channel_id=1, source_target_pairs={{0,192},{64,0},{128,64},{192,128},{1,193},{65,1},{129,65},{193,129... | collective-permute-start | bytes 786440 | tf_op jit(solution)/shard_map/ppermute | solution.py:446
  35.0 23.9 %collective-permute-start.13 = (bf16[512,256]{1,0:T(8,128)(2,1)S(1)}, bf16[512,256]{1,0:T(8,128)(2,1)S(1)}, u32[]{:S(2)}, u32[]{:S(2)}) collective-permute-start(bf16[512,256]{1,0:T(8,128)(2,1)S(1)} %pick_rows.3.refs_0_), channel_id=1, source_target_pairs={{0,64},{64,128},{128,192},{192,0},{1,65},{65,129},{129,193},{193,1... | collective-permute-start | bytes 786440 | tf_op jit(solution)/shard_map/ppermute | solution.py:446
  35.9 23.0 %collective-permute-start.12 = (bf16[512,256]{1,0:T(8,128)(2,1)S(1)}, bf16[512,256]{1,0:T(8,128)(2,1)S(1)}, u32[]{:S(2)}, u32[]{:S(2)}) collective-permute-start(bf16[512,256]{1,0:T(8,128)(2,1)S(1)} %pick_rows.3.refs_0_), channel_id=1, source_target_pairs={{0,128},{64,192},{128,0},{192,64},{1,129},{65,193},{129,1},{193,65... | collective-permute-start | bytes 786440 | tf_op jit(solution)/shard_map/ppermute | solution.py:446
  37.8 1.3 collective-permute-start.8
  37.8 1.5 collective-permute-start.7
  165.3 28.0 %all-to-all-start.7 = ((bf16[16,128,256]{2,1,0:T(8,128)(2,1)}), bf16[16,128,256]{2,1,0:T(8,128)(2,1)S(1)}, u32[]{:S(2)}, u32[]{:S(2)}) async-start(bf16[16,128,256]{2,1,0:T(8,128)(2,1)} %bitcast.3), calls=%async_computation.7 | async-start | bytes 2097152 | tf_op jit(solution)/shard_map/all_to_all | solution.py:463
  170.2 1.9 collective-permute-start.15
  170.2 1.9 collective-permute-start.16
  172.2 9.0 %collective-permute-start.17 = (bf16[144,256]{1,0:T(8,128)(2,1)S(1)}, bf16[144,256]{1,0:T(8,128)(2,1)S(1)}, u32[]{:S(2)}, u32[]{:S(2)}) collective-permute-start(bf16[144,256]{1,0:T(8,128)(2,1)S(1)} %get-tuple-element.66), channel_id=1, source_target_pairs={{0,8},{8,16},{16,24},{24,32},{32,40},{40,48},{48,56},{56,0},{1,9},... | collective-permute-start | bytes 221192 | tf_op jit(solution)/shard_map/ppermute | solution.py:450
  172.6 10.7 %collective-permute-start.18 = (bf16[144,256]{1,0:T(8,128)(2,1)S(1)}, bf16[144,256]{1,0:T(8,128)(2,1)S(1)}, u32[]{:S(2)}, u32[]{:S(2)}) collective-permute-start(bf16[144,256]{1,0:T(8,128)(2,1)S(1)} %get-tuple-element.67), channel_id=1, source_target_pairs={{0,16},{8,24},{16,32},{24,40},{32,48},{40,56},{48,0},{56,8},{1,17}... | collective-permute-start | bytes 221192 | tf_op jit(solution)/shard_map/ppermute | solution.py:450
  173.6 12.9 %collective-permute-start.19 = (bf16[144,256]{1,0:T(8,128)(2,1)S(1)}, bf16[144,256]{1,0:T(8,128)(2,1)S(1)}, u32[]{:S(2)}, u32[]{:S(2)}) collective-permute-start(bf16[144,256]{1,0:T(8,128)(2,1)S(1)} %get-tuple-element.68), channel_id=1, source_target_pairs={{0,24},{8,32},{16,40},{24,48},{32,56},{40,0},{48,8},{56,16},{1,25}... | collective-permute-start | bytes 221192 | tf_op jit(solution)/shard_map/ppermute | solution.py:450
  175.8 10.7 %collective-permute-start.20 = (bf16[144,256]{1,0:T(8,128)(2,1)S(1)}, bf16[144,256]{1,0:T(8,128)(2,1)S(1)}, u32[]{:S(2)}, u32[]{:S(2)}) collective-permute-start(bf16[144,256]{1,0:T(8,128)(2,1)S(1)} %get-tuple-element.69), channel_id=1, source_target_pairs={{0,32},{8,40},{16,48},{24,56},{32,0},{40,8},{48,16},{56,24},{1,33}... | collective-permute-start | bytes 221192 | tf_op jit(solution)/shard_map/ppermute | solution.py:450
  179.3 9.2 %collective-permute-start.21 = (bf16[144,256]{1,0:T(8,128)(2,1)S(1)}, bf16[144,256]{1,0:T(8,128)(2,1)S(1)}, u32[]{:S(2)}, u32[]{:S(2)}) collective-permute-start(bf16[144,256]{1,0:T(8,128)(2,1)S(1)} %get-tuple-element.70), channel_id=1, source_target_pairs={{0,40},{8,48},{16,56},{24,0},{32,8},{40,16},{48,24},{56,32},{1,41}... | collective-permute-start | bytes 221192 | tf_op jit(solution)/shard_map/ppermute | solution.py:450
  181.2 11.7 %collective-permute-start.22 = (bf16[144,256]{1,0:T(8,128)(2,1)S(1)}, bf16[144,256]{1,0:T(8,128)(2,1)S(1)}, u32[]{:S(2)}, u32[]{:S(2)}) collective-permute-start(bf16[144,256]{1,0:T(8,128)(2,1)S(1)} %get-tuple-element.71), channel_id=1, source_target_pairs={{0,48},{8,56},{16,0},{24,8},{32,16},{40,24},{48,32},{56,40},{1,49}... | collective-permute-start | bytes 221192 | tf_op jit(solution)/shard_map/ppermute | solution.py:450
  183.3 9.9 %collective-permute-start.23 = (bf16[144,256]{1,0:T(8,128)(2,1)S(1)}, bf16[144,256]{1,0:T(8,128)(2,1)S(1)}, u32[]{:S(2)}, u32[]{:S(2)}) collective-permute-start(bf16[144,256]{1,0:T(8,128)(2,1)S(1)} %get-tuple-element.72), channel_id=1, source_target_pairs={{0,56},{8,0},{16,8},{24,16},{32,24},{40,32},{48,40},{56,48},{1,57}... | collective-permute-start | bytes 221192 | tf_op jit(solution)/shard_map/ppermute | solution.py:450
  194.1 10.0 %all-to-all-start.8 = ((bf16[4,128,256]{2,1,0:T(8,128)(2,1)}), bf16[4,128,256]{2,1,0:T(8,128)(2,1)S(1)}, u32[]{:S(2)}, u32[]{:S(2)}) async-start(bf16[4,128,256]{2,1,0:T(8,128)(2,1)} %broadcast_in_dim.2), calls=%async_computation.8 | async-start | bytes 524288 | tf_op jit(solution)/shard_map/all_to_all | solution.py:471
